TPU v7x, 32 devices: a whole 2x2x4 slice. The times are simulated.
32 devices in a mesh: pp: 4 (over x, core), cp: 4 (over z), tp: 2 (over y).
Axes of the slice: x: 2, y: 2, z: 4, core: 2. Of those that a mesh axis runs over, the one named last changes fastest.
Arguments:
- query: bfloat16 [4, 512, 4096], P('pp', 'cp', 'tp'), may hold values from -200 to 200
- key: bfloat16 [4, 512, 256], P('pp', 'cp', 'tp'), may hold values from -6 to 6
- value: bfloat16 [4, 512, 256], P('pp', 'cp', 'tp'), may hold values from -6 to 6
- out_grad: bfloat16 [4, 512, 4096], P('pp', 'cp', 'tp'), may hold values from -24 to 24
- lengths: int32 [6], replicated, may hold values from 1 to 256, 512 in all
- plan: int32 [4, 4], replicated, may hold values from 0 to 3, each once within a row
Outputs:
- handed_grad: bfloat16 [4, 512, 4096], P('pp', 'cp', 'tp')
- key_grad: bfloat16 [4, 512, 256], P('pp', 'cp', 'tp')
- value_grad: bfloat16 [4, 512, 256], P('pp', 'cp', 'tp')
Inputs may be any that keep to these rules, and one draw needn't show every extreme that they name: Row s of plan is a permutation: for each of the blocks of 32 tokens of context shard s it names the shard that takes the block.
All inputs are finite; a program needn't handle non-finite values.
Results may differ from a plain program's by a relative error of at most 0.0085.
Values may be sent and summed in bfloat16 or wider, within the bound.
A program may use at most 64 MiB of HBM per device.

v0:
```python
import jax
import jax.numpy as jnp
from jax import lax
from jax.sharding import PartitionSpec as P


def passed_along(array, axis, by):
    peers = lax.axis_size(axis)
    pairs = [(i, i + by) for i in range(peers) if 0 <= i + by < peers]
    return lax.ppermute(array, axis, pairs)


def attend(query_rows, grad_rows, query_pos, key_full, value_full, owner):
    tokens = query_rows.shape[0]
    head_width = key_full.shape[1]
    head_count = query_rows.shape[1] // head_width
    key_count = key_full.shape[0]
    total_rows = tokens * head_count
    score_scale = head_width ** (-0.5)
    flat_query = query_rows.reshape(total_rows, head_width)
    flat_grad = grad_rows.reshape(total_rows, head_width)
    row_pos = jnp.repeat(query_pos, head_count)
    row_doc = jnp.repeat(jnp.take(owner, query_pos), head_count)
    block_width = min(512, key_count)
    block_count = key_count // block_width
    key_pos = jnp.arange(key_count, dtype=jnp.int32)
    blocks = (
        key_full.reshape(block_count, block_width, head_width),
        value_full.reshape(block_count, block_width, head_width),
        key_pos.reshape(block_count, block_width),
        owner.reshape(block_count, block_width),
    )

    def masked_scores(key_block, pos_block, doc_block):
        scores = jnp.dot(flat_query, key_block.T, preferred_element_type=jnp.float32) * score_scale
        seen = (doc_block[None, :] == row_doc[:, None]) & (pos_block[None, :] <= row_pos[:, None])
        return jnp.where(seen, scores, -jnp.inf)

    def first_pass(state, block):
        top, total, weighted = state
        key_block, value_block, pos_block, doc_block = block
        scores = masked_scores(key_block, pos_block, doc_block)
        new_top = jnp.maximum(top, jnp.max(scores, axis=1))
        expo = jnp.exp(scores - new_top[:, None])
        shrink = jnp.exp(top - new_top)
        dprob = jnp.dot(flat_grad, value_block.T, preferred_element_type=jnp.float32)
        total = total * shrink + jnp.sum(expo, axis=1)
        weighted = weighted * shrink + jnp.sum(expo * dprob, axis=1)
        return ((new_top, total, weighted), None)

    start = (
        jnp.full((total_rows,), -1e30, jnp.float32),
        jnp.zeros((total_rows,), jnp.float32),
        jnp.zeros((total_rows,), jnp.float32),
    )
    (top, total, weighted), unused = lax.scan(first_pass, start, blocks)
    delta = weighted / total

    def second_pass(dquery, block):
        key_block, value_block, pos_block, doc_block = block
        scores = masked_scores(key_block, pos_block, doc_block)
        probs = jnp.exp(scores - top[:, None]) / total[:, None]
        dprob = jnp.dot(flat_grad, value_block.T, preferred_element_type=jnp.float32)
        probs_low = probs.astype(jnp.bfloat16)
        dscore = (probs * (dprob - delta[:, None]) * score_scale).astype(jnp.bfloat16)
        dvalue = jnp.dot(probs_low.T, flat_grad, preferred_element_type=jnp.float32)
        dkey = jnp.dot(dscore.T, flat_query, preferred_element_type=jnp.float32)
        dquery = dquery + jnp.dot(dscore, key_block, preferred_element_type=jnp.float32)
        return (dquery, jnp.concatenate([dkey, dvalue], axis=1))

    dquery, terms = lax.scan(second_pass, jnp.zeros((total_rows, head_width), jnp.float32), blocks)
    dquery = dquery.astype(jnp.bfloat16).reshape(tokens, head_count * head_width)
    return (dquery, terms.reshape(key_count, 2 * head_width))


def body(query, key, value, out_grad, lengths, plan):
    tokens = query.shape[1]
    width = query.shape[2]
    head_width = key.shape[2]
    shards = lax.axis_size("cp")
    own_index = lax.axis_index("cp")
    block_rows = tokens // shards
    key_full, value_full = (
        lax.all_gather(key[0], "cp", axis=0, tiled=True),
        lax.all_gather(value[0], "cp", axis=0, tiled=True),
    )
    key_count = key_full.shape[0]
    ends = jnp.cumsum(lengths)
    positions = jnp.arange(key_count, dtype=jnp.int32)
    owner = jnp.sum((positions[:, None] >= ends[None, :]).astype(jnp.int32), axis=1)
    iota = jnp.arange(shards, dtype=jnp.int32)
    inverse = jnp.sum(
        (plan[:, None, :] == iota[None, :, None]).astype(jnp.int32) * iota[None, None, :], axis=2
    )
    send_order = lax.dynamic_index_in_dim(inverse, own_index, 0, keepdims=False)

    def reorder(rows):
        grouped = rows.reshape(shards, block_rows, rows.shape[1])
        return jnp.take(grouped, send_order, axis=0)

    query_sent, grad_sent = (
        lax.all_to_all(reorder(query[0]), "cp", split_axis=0, concat_axis=0, tiled=True),
        lax.all_to_all(reorder(out_grad[0]), "cp", split_axis=0, concat_axis=0, tiled=True),
    )
    taken = lax.dynamic_index_in_dim(inverse, own_index, 1, keepdims=False)
    query_pos = (
        iota[:, None] * tokens
        + taken[:, None] * block_rows
        + jnp.arange(block_rows, dtype=jnp.int32)[None, :]
    ).reshape(tokens)
    dquery, terms = attend(
        query_sent.reshape(tokens, width),
        grad_sent.reshape(tokens, width),
        query_pos,
        key_full,
        value_full,
        owner,
    )
    handed = passed_along(dquery, "pp", -1)
    summed = lax.psum_scatter(terms, "cp", scatter_dimension=0, tiled=True)
    key_grad = summed[:, :head_width].astype(jnp.bfloat16)
    value_grad = summed[:, head_width:].astype(jnp.bfloat16)
    return (handed[None], key_grad[None], value_grad[None])


def solution(mesh):
    return jax.shard_map(
        body,
        mesh=mesh,
        in_specs=(
            P("pp", "cp", "tp"),
            P("pp", "cp", "tp"),
            P("pp", "cp", "tp"),
            P("pp", "cp", "tp"),
            P(),
            P(),
        ),
        out_specs=(P("pp", "cp", "tp"), P("pp", "cp", "tp"), P("pp", "cp", "tp")),
        check_vma=False,
    )
```

profile of v0, /device:TPU:0, one launch (start us, length us, event | category | flops | bytes accessed | tf_op | source)
XLA Modules:
  0.0 112.5 jit_solution(1068938269097290352)
XLA Ops:
  7.2 0.9 select_reduce_fusion
  8.1 0.1 copy-done
  8.2 0.6 gather_fusion.2
  8.8 1.6 %gather_fusion.1 = bf16[4,32,2048]{2,1,0:T(8,128)(2,1)S(1)} fusion(bf16[4,32,2048]{2,1,0:T(8,128)(2,1)} %bitcast.34, s32[1024]{0:T(1024)S(1)} %pad_clamp_fusion), kind=kCustom, calls=%fused_computation.clone | custom fusion | bytes 1048592 | tf_op jit(solution)/shard_map/jit(_take)/gather | solution.py:99
  10.4 1.1 %broadcast_select_fusion.1 = (bf16[4,32,2048]{2,1,0:T(8,128)(2,1)}, bf16[4,32,2048]{2,1,0:T(8,128)(2,1)}) fusion(bf16[4,32,2048]{2,1,0:T(8,128)(2,1)S(1)} %gather_fusion.1, pred[4]{0:T(512)(128)(4,1)S(1)} %get-tuple-element.79, bf16[4,32,2048]{2,1,0:T(8,128)(2,1)S(1)} %gather_fusion.2), kind=kLoop, calls=%fused_computation.16 | loop fusion | flops 524288 | bytes 2097156 | tf_op jit(solution)/shard_map/jit(_take)/select_n | solution.py:99
  11.6 6.3 %all-to-all-start = ((bf16[4,32,2048]{2,1,0:T(8,128)(2,1)}), bf16[4,32,2048]{2,1,0:T(8,128)(2,1)S(1)}, u32[]{:S(2)}, u32[]{:S(2)}) async-start(bf16[4,32,2048]{2,1,0:T(8,128)(2,1)} %get-tuple-element.85), calls=%async_computation | async-start | bytes 1048576 | tf_op jit(solution)/shard_map/all_to_all | solution.py:102
  17.9 0.2 add_reduce_fusion
  18.3 0.2 reduce-window.8
  18.6 0.1 le.54
  18.8 1.3 %gather_fusion = s32[128]{0:T(128)S(1)} fusion(s32[512]{0:T(512)S(1)} %convert_reduce_fusion, s32[1024]{0:T(1024)S(1)} %pad_clamp_fusion.1), kind=kCustom, calls=%fused_computation.2 | custom fusion | bytes 1536 | tf_op jit(solution)/shard_map/jit(_take)/gather | solution.py:23
  20.1 12.3 %all-to-all-done = bf16[4,32,2048]{2,1,0:T(8,128)(2,1)S(1)} async-done(((bf16[4,32,2048]{2,1,0:T(8,128)(2,1)}), bf16[4,32,2048]{2,1,0:T(8,128)(2,1)S(1)}, u32[]{:S(2)}, u32[]{:S(2)}) %all-to-all-start) | async-done | bytes 524320 | tf_op jit(solution)/shard_map/all_to_all | solution.py:102
  32.4 3.5 %all-to-all-start.1 = ((bf16[4,32,2048]{2,1,0:T(8,128)(2,1)}), bf16[4,32,2048]{2,1,0:T(8,128)(2,1)S(1)}, u32[]{:S(2)}, u32[]{:S(2)}) async-start(bf16[4,32,2048]{2,1,0:T(8,128)(2,1)} %get-tuple-element.86), calls=%async_computation.1 | async-start | bytes 1048576 | tf_op jit(solution)/shard_map/all_to_all | solution.py:103
  36.0 0.1 eq.53
  36.1 20.2 %all-gather = bf16[1,512,128]{2,1,0:T(8,128)(2,1)S(1)} all-gather(bf16[1,128,128]{2,1,0:T(8,128)(2,1)S(1)} %copy-done.2), channel_id=2, replica_groups=mesh['pp'=4,'cp'=4,'tp'=2] {'cp'}, dimensions={1}, use_global_device_ids=true | all-gather | bytes 163840 | tf_op jit(solution)/shard_map/all_gather | solution.py:84
  56.3 13.3 %all-gather.1 = bf16[1,512,128]{2,1,0:T(8,128)(2,1)S(1)} all-gather(bf16[1,128,128]{2,1,0:T(8,128)(2,1)S(1)} %copy-done.3), channel_id=3, replica_groups=mesh['pp'=4,'cp'=4,'tp'=2] {'cp'}, dimensions={1}, use_global_device_ids=true | all-gather | bytes 163840 | tf_op jit(solution)/shard_map/all_gather | solution.py:85
  69.6 0.2 reshape_reshape.6
  69.8 3.1 %fusion.12 = (f32[2048]{0:T(1024)S(1)}, f32[2048,512]{0,1:T(8,128)}) fusion(bf16[2048,128]{1,0:T(8,128)(2,1)S(1)} %reshape_reshape.6, bf16[1,512,128]{2,1,0:T(8,128)(2,1)S(1)} %all-gather, s32[2048]{0:T(1024)S(1)} %le.54, s32[2048]{0:T(1024)S(1)} %eq.53, s32[512]{0:T(512)S(1)} %convert_reduce_fusion), kind=kOutput, calls=%fused_computation.41 | convolution fusion | flops 274724864 | bytes 4876288 | tf_op jit(solution)/shard_map/while/body/eval_jaxpr/dot_general | solution.py:35
  72.9 0.2 reshape_reshape.7
  73.2 3.3 %fusion.2 = (f32[2048]{0:T(1024)S(1)}, f32[2048]{0:T(1024)S(1)}, f32[2048,512]{0,1:T(8,128)S(1)}) fusion(f32[2048,512]{0,1:T(8,128)} %get-tuple-element.88, f32[2048]{0:T(1024)S(1)} %broadcast_maximum_fusion, bf16[2048,128]{1,0:T(8,128)(2,1)S(1)} %reshape_reshape.7, bf16[1,512,128]{2,1,0:T(8,128)(2,1)S(1)} %all-gather.1), kind=kOutput, calls=%fused_computation.10 | convolution fusion | flops 272625664 | bytes 9068544 | tf_op jit(solution)/shard_map/while/body/eval_jaxpr/dot_general | solution.py:63
  76.6 1.0 fusion.3
  77.6 1.1 %multiply_convert_fusion = bf16[2048,512]{0,1:T(8,128)(2,1)S(1)} fusion(f32[2048,512]{0,1:T(8,128)S(1)} %get-tuple-element.89, f32[2048]{0:T(1024)S(1)} %get-tuple-element.84, f32[2048]{0:T(1024)S(1)} %get-tuple-element.83, f32[2048,512]{0,1:T(8,128)S(1)} %copy-done.1, f32[2048]{0:T(1024)S(1)} %broadcast_maximum_fusion), kind=kLoop, calls=%fused_computation.3 | loop fusion | flops 6291456 | bytes 10510336 | tf_op jit(solution)/shard_map/while/body/eval_jaxpr/convert_element_type | solution.py:65
  78.7 0.8 fusion.13
  79.6 0.8 pad_maximum_fusion
  80.4 0.8 convolution_convert_fusion
  81.2 0.2 reshape.121
  81.4 1.3 %collective-permute-start = (bf16[128,2048]{1,0:T(8,128)(2,1)S(1)}, bf16[128,2048]{1,0:T(8,128)(2,1)S(1)}, u32[]{:S(2)}, u32[]{:S(2)}) collective-permute-start(bf16[128,2048]{1,0:T(8,128)(2,1)S(1)} %reshape.121), channel_id=1, source_target_pairs={{8,0},{16,8},{24,16},{9,1},{17,9},{25,17},{10,2},{18,10},{26,18},{... | collective-permute-start | bytes 1572872 | tf_op jit(solution)/shard_map/ppermute | solution.py:10
  82.7 2.5 %collective-permute-done = bf16[128,2048]{1,0:T(8,128)(2,1)S(1)} collective-permute-done((bf16[128,2048]{1,0:T(8,128)(2,1)S(1)}, bf16[128,2048]{1,0:T(8,128)(2,1)S(1)}, u32[]{:S(2)}, u32[]{:S(2)}) %collective-permute-start) | collective-permute-done | bytes 524320 | tf_op jit(solution)/shard_map/ppermute | solution.py:10
  85.2 17.3 %reduce-scatter.2.cloned.1.call-done = f32[128,256]{0,1:T(8,128)} async-done(((f32[512,256]{0,1:T(8,128)}), f32[128,256]{0,1:T(8,128)}) %reduce-scatter.2.cloned.1.call-update) | async-done | bytes 131088 | tf_op jit(solution)/shard_map/reduce_scatter | solution.py:120
  102.5 0.9 convert.4
  103.5 0.7 copy.14
  104.2 0.7 copy.13
  104.9 0.8 copy.16
  (26 shorter events, 0.7 us)
Async XLA Ops:
  7.2 1.1 copy-start
  7.2 11.1 %copy-start.4 = (s32[6]{0:T(128)S(1)}, s32[6]{0:T(128)}, u32[]{:S(2)}) copy-start(s32[6]{0:T(128)} %param.12) | copy-start | bytes 76
  7.2 28.9 %copy-start.2 = (bf16[1,128,128]{2,1,0:T(8,128)(2,1)S(1)}, bf16[1,128,128]{2,1,0:T(8,128)(2,1)}, u32[]{:S(2)}) copy-start(bf16[1,128,128]{2,1,0:T(8,128)(2,1)} %param.9) | copy-start | bytes 98308
  7.2 49.1 %copy-start.3 = (bf16[1,128,128]{2,1,0:T(8,128)(2,1)S(1)}, bf16[1,128,128]{2,1,0:T(8,128)(2,1)}, u32[]{:S(2)}) copy-start(bf16[1,128,128]{2,1,0:T(8,128)(2,1)} %param.10) | copy-start | bytes 98308
  11.6 20.8 %all-to-all-start = ((bf16[4,32,2048]{2,1,0:T(8,128)(2,1)}), bf16[4,32,2048]{2,1,0:T(8,128)(2,1)S(1)}, u32[]{:S(2)}, u32[]{:S(2)}) async-start(bf16[4,32,2048]{2,1,0:T(8,128)(2,1)} %get-tuple-element.85), calls=%async_computation | async-start | bytes 1048576 | tf_op jit(solution)/shard_map/all_to_all | solution.py:102
  32.4 40.5 %all-to-all-start.1 = ((bf16[4,32,2048]{2,1,0:T(8,128)(2,1)}), bf16[4,32,2048]{2,1,0:T(8,128)(2,1)S(1)}, u32[]{:S(2)}, u32[]{:S(2)}) async-start(bf16[4,32,2048]{2,1,0:T(8,128)(2,1)} %get-tuple-element.86), calls=%async_computation.1 | async-start | bytes 1048576 | tf_op jit(solution)/shard_map/all_to_all | solution.py:103
  35.9 66.7 %reduce-scatter.2.cloned.1.call-start = ((), (), s32[]{:S(2)}) async-start(), calls=%async_computation.3 | async-start | bytes 655360 | tf_op jit(solution)/shard_map/reduce_scatter | solution.py:120
  73.2 3.5 %copy-start.1 = (f32[2048,512]{0,1:T(8,128)S(1)}, f32[2048,512]{0,1:T(8,128)}, u32[]{:S(2)}) copy-start(f32[2048,512]{0,1:T(8,128)} %get-tuple-element.88) | copy-start | bytes 12582916
  81.4 3.8 %collective-permute-start = (bf16[128,2048]{1,0:T(8,128)(2,1)S(1)}, bf16[128,2048]{1,0:T(8,128)(2,1)S(1)}, u32[]{:S(2)}, u32[]{:S(2)}) collective-permute-start(bf16[128,2048]{1,0:T(8,128)(2,1)S(1)} %reshape.121), channel_id=1, source_target_pairs={{8,0},{16,8},{24,16},{9,1},{17,9},{25,17},{10,2},{18,10},{26,18},{... | collective-permute-start | bytes 1572872 | tf_op jit(solution)/shard_map/ppermute | solution.py:10
Sparse Core Ops, SparseCore 0:
  80.5 21.9 reduce-scatter.1
where the time goes:
time: 113 us
  blocking collectives  33.5 us (30%)
  waiting for transfers between devices  32.2 us (28%)
  between operations  14.2 us (13%)
  starting transfers between devices  11.1 us (10%)
  matrix products  8.98 us (8%)
  local copies, waits for them, and re-layouts  7.11 us (6%)
  other arithmetic  5.46 us (5%)
    all_gather x1, blocking collectives, body(): lax.all_gather(key[0], 'cp', axis=0, tiled=True)  20.2 us
    reduce_scatter x1, waiting for transfers between devices, body(): summed = lax.psum_scatter(terms, 'cp', scatter_dimension=0, tiled=True)  17.3 us
    all_gather x1, blocking collectives, body(): lax.all_gather(value[0], 'cp', axis=0, tiled=True)  13.3 us
    all_to_all x1, waiting for transfers between devices, body(): lax.all_to_all(reorder(query[0]), 'cp', split_axis=0, concat_axis=0, tile...  12.3 us
    all_to_all x1, starting transfers between devices, body(): lax.all_to_all(reorder(query[0]), 'cp', split_axis=0, concat_axis=0, tile...  6.32 us
    all_to_all x1, starting transfers between devices, body(): lax.all_to_all(reorder(out_grad[0]), 'cp', split_axis=0, concat_axis=0, t...  3.47 us
    dot_general x1, matrix products, second_pass(): jnp.dot(flat_grad, value_block.T, preferred_element_type=jnp.float32)  3.35 us
    dot_general x1, matrix products, masked_scores(): jnp.dot(flat_query, key_block.T, preferred_element_type=jnp.float32)  3.07 us
  transfers between devices with their start and end apart: 4, of which 3 were waited for; matrix products, arithmetic and copies ran while one was open for 6% of the time, Pallas kernels for 0%

commit v1 on v0

v1 whole, which is shorter than its diff:
```python
import functools
import math

import jax
import jax.numpy as jnp
from jax import lax
from jax.experimental import pallas as pl
from jax.experimental.pallas import tpu as pltpu
from jax.sharding import PartitionSpec as P

MESH = pl.DeviceIdType.MESH
F32 = jnp.float32
BF16 = jnp.bfloat16
NT = (((1,), (1,)), ((), ()))


def kernel(
    sizes,
    plan_ref, lens_ref, q_hbm, k_hbm, v_hbm, g_hbm,
    handed, kg_ref, vg_ref,
    qraw, graw, qs, gs, kall, vall, kt, bias, pst, dst, stag, zero, dsend, drecv, acc,
    in_sem, own_sem, kv_send, kv_recv, dq_send, dq_recv, d_send, d_recv, zero_sem,
):
    n_pp, n_cp, tokens, heads, nkv, hd, ndoc, groups, chunk = sizes
    group_heads = heads // nkv
    per_group = n_cp // groups
    block_rows = tokens // n_cp
    me = lax.axis_index("cp")
    sec = lax.axis_index("pp")
    my_group = me // per_group
    scale = hd ** -0.5

    q_in = pltpu.make_async_copy(q_hbm.at[0], qraw, in_sem.at[0])
    g_in = pltpu.make_async_copy(g_hbm.at[0], graw, in_sem.at[1])
    q_in.start()
    g_in.start()
    my_rows = pl.ds(pl.multiple_of(me * tokens, tokens), tokens)
    k_own = pltpu.make_async_copy(k_hbm.at[0], kall.at[my_rows], own_sem.at[0])
    v_own = pltpu.make_async_copy(v_hbm.at[0], vall.at[my_rows], own_sem.at[1])
    k_own.start()
    v_own.start()

    barrier = pltpu.get_barrier_semaphore()
    for d in range(n_cp):
        @pl.when(me != d)
        def _():
            pl.semaphore_signal(barrier, inc=1, device_id={"cp": d}, device_id_type=MESH)

        @pl.when(sec < n_pp - 1)
        def _():
            pl.semaphore_signal(barrier, inc=1, device_id={"pp": sec + 1, "cp": d}, device_id_type=MESH)

    @pl.when(sec > 0)
    def _():
        pl.semaphore_wait(barrier, 2 * n_cp - 1)

    @pl.when(sec == 0)
    def _():
        pl.semaphore_wait(barrier, n_cp - 1)

    def kv_copies(d, source):
        rows = pl.ds(pl.multiple_of(source * tokens, tokens), tokens)
        return [
            pltpu.make_async_remote_copy(
                src_ref=hbm.at[0], dst_ref=full.at[rows],
                send_sem=kv_send.at[i, d], recv_sem=kv_recv.at[i, source],
                device_id={"cp": d}, device_id_type=MESH,
            )
            for i, (hbm, full) in enumerate(((k_hbm, kall), (v_hbm, vall)))
        ]

    for d in reversed(range(n_cp)):
        @pl.when((me != d) & (my_group <= d // per_group))
        def _():
            for copy in kv_copies(d, me):
                copy.start()

    @pl.when(sec == n_pp - 1)
    def _():
        zero[...] = jnp.zeros_like(zero)
        pltpu.make_async_copy(zero, handed.at[0], zero_sem).start()

    def taken_of(slot):
        taken = jnp.zeros_like(slot)
        for d in range(n_cp):
            inverse = jnp.int32(0)
            for j in range(1, n_cp):
                inverse = inverse + jnp.where(plan_ref[me, j] == d, j, 0)
            taken = jnp.where(slot == d, inverse, taken)
        return taken

    row = lax.broadcasted_iota(jnp.int32, (tokens, tokens), 0)
    col = lax.broadcasted_iota(jnp.int32, (tokens, tokens), 1)
    row_slot = row // block_rows
    local = taken_of(row_slot) * block_rows + (row - row_slot * block_rows)
    perm = jnp.where(local == col, 1.0, 0.0).astype(BF16)

    lane = lax.broadcasted_iota(jnp.int32, (1, tokens), 1)
    lane_slot = lane // block_rows
    q_pos = me * tokens + taken_of(lane_slot) * block_rows + (lane - lane_slot * block_rows)
    begin = jnp.zeros_like(q_pos)
    end = jnp.int32(0)
    for i in range(ndoc):
        end = end + lens_ref[i]
        begin = jnp.where(q_pos >= end, end, begin)
    for s in range(n_cp):
        k_pos = lax.broadcasted_iota(jnp.int32, (tokens, tokens), 0) + s * tokens
        seen = (k_pos >= begin) & (k_pos <= q_pos)
        bias[s * tokens:(s + 1) * tokens, :] = jnp.where(seen, 0.0, -jnp.inf)

    q_in.wait()
    g_in.wait()

    def stack(raw, out, c):
        width = 4 * hd
        cols = pl.ds(pl.multiple_of(c * width, width), width)
        moved = jnp.dot(perm, raw[:, cols], preferred_element_type=F32).astype(BF16)
        for h in range(4):
            at = pl.ds(pl.multiple_of((c * 4 + h) * tokens, tokens), tokens)
            out[at, :] = moved[:, h * hd:(h + 1) * hd]

    def stack_both(c, carry):
        stack(qraw, qs, c)
        stack(graw, gs, c)
        return carry

    lax.fori_loop(0, heads // 4, stack_both, 0)
    k_own.wait()
    v_own.wait()

    def dq_copy(d, cols):
        return pltpu.make_async_remote_copy(
            src_ref=stag.at[pl.ds(d * block_rows, block_rows), cols],
            dst_ref=handed.at[0, pl.ds(pl.multiple_of(me * block_rows, block_rows), block_rows), cols],
            send_sem=dq_send, recv_sem=dq_recv,
            device_id={"pp": sec - 1, "cp": d}, device_id_type=MESH,
        )

    def d_copy(kb, source, cols):
        at = pl.ds(pl.multiple_of(source * tokens, tokens), tokens)
        return pltpu.make_async_remote_copy(
            src_ref=dsend.at[pl.ds(kb * tokens, tokens), cols],
            dst_ref=drecv.at[at, cols],
            send_sem=d_send.at[kb], recv_sem=d_recv.at[source],
            device_id={"cp": kb}, device_id_type=MESH,
        )

    def work(group):
        shards = (group + 1) * per_group
        count = shards * tokens
        for s in range(shards):
            @pl.when(me != s)
            def _():
                for copy in kv_copies(s, s):
                    copy.wait_recv()

        def one_kv(kv, carry):
            kv_cols = pl.ds(pl.multiple_of(kv * hd, hd), hd)
            for s in range(shards):
                at = slice(s * tokens, (s + 1) * tokens)
                kt[:, at] = kall[at, kv_cols].astype(F32).T.astype(BF16)

            def one_chunk(c, carry):
                for pair in range(chunk // 2):
                    first = c * chunk + pair * 2
                    rows = pl.ds(pl.multiple_of((kv * group_heads + first) * tokens, 2 * tokens), 2 * tokens)
                    kept = pl.ds(pl.multiple_of(first * tokens, 2 * tokens), 2 * tokens)
                    seen = bias[0:count, :]
                    score = lax.dot_general(kall[0:count, kv_cols], qs[rows, :], NT, preferred_element_type=F32)
                    score = score + jnp.concatenate([seen, seen], axis=1)
                    dprob = lax.dot_general(vall[0:count, kv_cols], gs[rows, :], NT, preferred_element_type=F32)
                    top = jnp.max(score, axis=0, keepdims=True)
                    expo = jnp.exp2((score - top) * (scale * math.log2(math.e)))
                    inverse = 1.0 / jnp.sum(expo, axis=0, keepdims=True)
                    delta = jnp.sum(expo * dprob, axis=0, keepdims=True) * inverse
                    pst[0:count, kept] = (expo * inverse).astype(BF16)
                    dscore = (expo * (inverse * scale) * (dprob - delta)).astype(BF16)
                    dst[0:count, kept] = dscore

                    @pl.when(sec > 0)
                    def _():
                        dqt = jnp.dot(kt[:, 0:count], dscore, preferred_element_type=F32)
                        for h in range(2):
                            at = pl.ds(pl.multiple_of((kv * group_heads + first + h) * hd, hd), hd)
                            stag[:, at] = dqt[:, h * tokens:(h + 1) * tokens].T.astype(stag.dtype)

                @pl.when(sec > 0)
                def _():
                    width = chunk * hd
                    cols = pl.ds(pl.multiple_of(kv * group_heads * hd + c * width, width), width)
                    for d in range(n_cp):
                        dq_copy(d, cols).start()

                return carry

            lax.fori_loop(0, group_heads // chunk, one_chunk, 0)

            all_rows = pl.ds(pl.multiple_of(kv * group_heads * tokens, group_heads * tokens), group_heads * tokens)
            term_cols = pl.ds(pl.multiple_of(kv * 2 * hd, 2 * hd), 2 * hd)
            for kb in range(shards):
                at = slice(kb * tokens, (kb + 1) * tokens)
                dkey = jnp.dot(dst[at, :], qs[all_rows, :], preferred_element_type=F32)
                dvalue = jnp.dot(pst[at, :], gs[all_rows, :], preferred_element_type=F32)
                both = jnp.concatenate([dkey, dvalue], axis=1)

                @pl.when(me == kb)
                def _():
                    acc[:, term_cols] = both

                @pl.when(me != kb)
                def _():
                    dsend[at, term_cols] = both.astype(BF16)
                    d_copy(kb, me, term_cols).start()

            return carry

        if nkv == 1:
            one_kv(0, 0)
        else:
            lax.fori_loop(0, nkv, one_kv, 0)

    for group in range(groups):
        pl.when(my_group == group)(functools.partial(work, group))

    everything = pl.ds(0, nkv * 2 * hd)
    for s in range(n_cp):
        @pl.when((me != s) & (my_group <= s // per_group))
        def _():
            d_copy(0, s, everything).wait_recv()
            acc[...] += drecv[s * tokens:(s + 1) * tokens, :].astype(F32)

    for kv in range(nkv):
        kg_ref[0, :, kv * hd:(kv + 1) * hd] = acc[:, kv * 2 * hd:kv * 2 * hd + hd].astype(BF16)
        vg_ref[0, :, kv * hd:(kv + 1) * hd] = acc[:, kv * 2 * hd + hd:(kv + 1) * 2 * hd].astype(BF16)

    for d in range(n_cp):
        @pl.when((me != d) & (my_group <= d // per_group))
        def _():
            for copy in kv_copies(d, me):
                copy.wait_send()

        @pl.when((me != d) & (my_group >= d // per_group))
        def _():
            d_copy(d, me, everything).wait_send()

    whole = pltpu.make_async_remote_copy(
        src_ref=stag, dst_ref=handed.at[0], send_sem=dq_send, recv_sem=dq_recv,
        device_id={"pp": lax.rem(sec + 1, n_pp)}, device_id_type=MESH,
    )

    @pl.when(sec > 0)
    def _():
        whole.wait_send()

    @pl.when(sec < n_pp - 1)
    def _():
        whole.wait_recv()

    @pl.when(sec == n_pp - 1)
    def _():
        pltpu.make_async_copy(zero, handed.at[0], zero_sem).wait()


def body(n_pp, n_cp, n_tp, query, key, value, out_grad, lengths, plan):
    tokens, width = query.shape[1], query.shape[2]
    kv_width = key.shape[2]
    hd = 128
    heads, nkv = width // hd, kv_width // hd
    groups = min(n_cp, 4)
    block_rows = tokens // n_cp
    seq = n_cp * tokens
    wide = BF16 if block_rows % 16 == 0 else F32
    chunk = 4
    group_rows = heads // nkv * tokens
    sizes = (n_pp, n_cp, tokens, heads, nkv, hd, lengths.shape[0], groups, chunk)
    anywhere = pl.BlockSpec(memory_space=pl.ANY)
    vmem = pl.BlockSpec(memory_space=pltpu.VMEM)
    smem = pl.BlockSpec(memory_space=pltpu.SMEM)
    dma = pltpu.SemaphoreType.DMA
    handed, key_grad, value_grad = pl.pallas_call(
        functools.partial(kernel, sizes),
        out_shape=(
            jax.ShapeDtypeStruct(query.shape, wide),
            jax.ShapeDtypeStruct(key.shape, BF16),
            jax.ShapeDtypeStruct(value.shape, BF16),
        ),
        in_specs=[smem, smem, anywhere, anywhere, anywhere, anywhere],
        out_specs=(anywhere, vmem, vmem),
        scratch_shapes=[
            pltpu.VMEM((tokens, width), BF16),
            pltpu.VMEM((tokens, width), BF16),
            pltpu.VMEM((heads * tokens, hd), BF16),
            pltpu.VMEM((heads * tokens, hd), BF16),
            pltpu.VMEM((seq, kv_width), BF16),
            pltpu.VMEM((seq, kv_width), BF16),
            pltpu.VMEM((hd, seq), BF16),
            pltpu.VMEM((seq, tokens), F32),
            pltpu.VMEM((seq, group_rows), BF16),
            pltpu.VMEM((seq, group_rows), BF16),
            pltpu.VMEM((tokens, width), wide),
            pltpu.VMEM((tokens, width), wide),
            pltpu.VMEM((seq, 2 * kv_width), BF16),
            pltpu.VMEM((seq, 2 * kv_width), BF16),
            pltpu.VMEM((tokens, 2 * kv_width), F32),
            dma((2,)), dma((2,)), dma((2, n_cp)), dma((2, n_cp)),
            dma, dma, dma((n_cp,)), dma((n_cp,)), dma,
        ],
        compiler_params=pltpu.CompilerParams(
            collective_id=0, has_side_effects=True, vmem_limit_bytes=(56 if seq > 512 else 32) * 2 ** 20
        ),
        cost_estimate=pl.CostEstimate(
            flops=10 * tokens * heads * seq * hd, bytes_accessed=6 * tokens * width,
            transcendentals=tokens * heads * seq,
        ),
    )(plan, lengths, query, key, value, out_grad)
    return handed.astype(BF16), key_grad, value_grad


def solution(mesh):
    spec = P("pp", "cp", "tp")
    sizes = (mesh.shape["pp"], mesh.shape["cp"], mesh.shape["tp"])
    return jax.shard_map(
        functools.partial(body, *sizes),
        mesh=mesh,
        in_specs=(spec, spec, spec, spec, P(), P()),
        out_specs=(spec, spec, spec),
        check_vma=False,
    )
```

time: 113 us -> 38.7 us (0.34)
  the two profiles are of different devices: /device:TPU:0 before, /device:TPU:2 now
where the time goes in v1:
time: 38.7 us; the launch traced here: 38.3 us
  Pallas kernels  30.7 us (79%)
  local copies, waits for them, and re-layouts  6.95 us (18%)
  between operations  0.65 us (2%)
    pallas_call x1, Pallas kernels, body(): pl.pallas_call(functools.partial(kernel, sizes), out_shape=(jax.ShapeDtyp...  30.7 us
    unnamed x15, local copies, waits for them, and re-layouts  6.95 us

profile of v1, /device:TPU:2, one launch (start us, length us, event | category | flops | bytes accessed | tf_op | source)
XLA Modules:
  0.0 38.3 jit_solution(14336583661263298839)
XLA Ops:
  0.6 0.0 copy-start
  0.6 1.0 %copy-done = bf16[1,128,2048]{2,1,0:T(8,128)(2,1)S(1)} copy-done((bf16[1,128,2048]{2,1,0:T(8,128)(2,1)S(1)}, bf16[1,128,2048]{2,1,0:T(8,128)(2,1)}, u32[]{:S(2)}) %copy-start) | copy-done | bytes 524312
  1.7 0.0 copy-start.1
  1.7 1.0 %copy-done.1 = bf16[1,128,2048]{2,1,0:T(8,128)(2,1)S(1)} copy-done((bf16[1,128,2048]{2,1,0:T(8,128)(2,1)S(1)}, bf16[1,128,2048]{2,1,0:T(8,128)(2,1)}, u32[]{:S(2)}) %copy-start.1) | copy-done | bytes 524312
  2.7 0.0 copy-start.2
  2.7 0.8 %copy-done.2 = bf16[1,128,128]{2,1,0:T(8,128)(2,1)S(1)} copy-done((bf16[1,128,128]{2,1,0:T(8,128)(2,1)S(1)}, bf16[1,128,128]{2,1,0:T(8,128)(2,1)}, u32[]{:S(2)}) %copy-start.2) | copy-done | bytes 32792
  3.5 0.0 copy-start.3
  3.5 0.8 %copy-done.3 = bf16[1,128,128]{2,1,0:T(8,128)(2,1)S(1)} copy-done((bf16[1,128,128]{2,1,0:T(8,128)(2,1)S(1)}, bf16[1,128,128]{2,1,0:T(8,128)(2,1)}, u32[]{:S(2)}) %copy-start.3) | copy-done | bytes 32792
  4.2 0.0 copy-start.4
  4.2 0.7 %copy-done.4 = s32[4,4]{1,0:T(4,128)S(1)} copy-done((s32[4,4]{1,0:T(4,128)S(1)}, s32[4,4]{1,0:T(4,128)}, u32[]{:S(2)}) %copy-start.4) | copy-done | bytes 88
  4.9 0.0 copy-start.5
  4.9 0.7 %copy-done.5 = s32[6]{0:T(128)S(1)} copy-done((s32[6]{0:T(128)S(1)}, s32[6]{0:T(128)}, u32[]{:S(2)}) %copy-start.5) | copy-done | bytes 48
  5.6 30.7 %shard_map.85 = (bf16[1,128,2048]{2,1,0:T(8,128)(2,1)S(1)}, bf16[1,128,128]{2,1,0:T(8,128)(2,1)S(1)}, bf16[1,128,128]{2,1,0:T(8,128)(2,1)S(1)}) custom-call(s32[4,4]{1,0:T(4,128)S(1)} %copy-done.4, s32[6]{0:T(128)S(1)} %copy-done.5, bf16[1,128,2048]{2,1,0:T(8,128)(2,1)S(1)} %copy-done, bf16[1,128,128]{2,1,0:T(8,128)(2,1)S(1)} %copy-done.2, ...), custom_call_target="tpu_custom_call" | custom-call | flops 1342177280 | bytes 1572864 | tf_op jit(solution)/shard_map/pallas_call | solution.py:280
  36.3 0.8 %copy.12 = bf16[1,128,2048]{2,1,0:T(8,128)(2,1)} copy(bf16[1,128,2048]{2,1,0:T(8,128)(2,1)S(1)} %get-tuple-element.6) | data formatting | bytes 1048576
  37.1 0.6 %copy.13 = bf16[1,128,128]{2,1,0:T(8,128)(2,1)} copy(bf16[1,128,128]{2,1,0:T(8,128)(2,1)S(1)} %get-tuple-element.7) | data formatting | bytes 65536
  37.7 0.6 %copy.14 = bf16[1,128,128]{2,1,0:T(8,128)(2,1)} copy(bf16[1,128,128]{2,1,0:T(8,128)(2,1)S(1)} %get-tuple-element.8) | data formatting | bytes 65536
Async XLA Ops:
  0.6 1.0 %copy-start = (bf16[1,128,2048]{2,1,0:T(8,128)(2,1)S(1)}, bf16[1,128,2048]{2,1,0:T(8,128)(2,1)}, u32[]{:S(2)}) copy-start(bf16[1,128,2048]{2,1,0:T(8,128)(2,1)} %q_hbm.1) | copy-start | bytes 1572868
  1.7 1.0 %copy-start.1 = (bf16[1,128,2048]{2,1,0:T(8,128)(2,1)S(1)}, bf16[1,128,2048]{2,1,0:T(8,128)(2,1)}, u32[]{:S(2)}) copy-start(bf16[1,128,2048]{2,1,0:T(8,128)(2,1)} %g_hbm.1) | copy-start | bytes 1572868
  2.7 0.8 %copy-start.2 = (bf16[1,128,128]{2,1,0:T(8,128)(2,1)S(1)}, bf16[1,128,128]{2,1,0:T(8,128)(2,1)}, u32[]{:S(2)}) copy-start(bf16[1,128,128]{2,1,0:T(8,128)(2,1)} %k_hbm.1) | copy-start | bytes 98308
  3.5 0.8 %copy-start.3 = (bf16[1,128,128]{2,1,0:T(8,128)(2,1)S(1)}, bf16[1,128,128]{2,1,0:T(8,128)(2,1)}, u32[]{:S(2)}) copy-start(bf16[1,128,128]{2,1,0:T(8,128)(2,1)} %v_hbm.1) | copy-start | bytes 98308
  4.2 0.7 %copy-start.4 = (s32[4,4]{1,0:T(4,128)S(1)}, s32[4,4]{1,0:T(4,128)}, u32[]{:S(2)}) copy-start(s32[4,4]{1,0:T(4,128)} %plan_ref.1) | copy-start | bytes 196
  4.9 0.7 %copy-start.5 = (s32[6]{0:T(128)S(1)}, s32[6]{0:T(128)}, u32[]{:S(2)}) copy-start(s32[6]{0:T(128)} %lens_ref.1) | copy-start | bytes 76

commit v2 on v1

--- a/solution.py
+++ b/solution.py
@@ -11,15 +11,16 @@
 MESH = pl.DeviceIdType.MESH
 F32 = jnp.float32
 BF16 = jnp.bfloat16
+VMEM = 60 * 2 ** 20
 NT = (((1,), (1,)), ((), ()))
 
 
 def kernel(
     sizes,
-    plan_ref, lens_ref, q_hbm, k_hbm, v_hbm, g_hbm,
+    plan_hbm, lens_hbm, q_hbm, k_hbm, v_hbm, g_hbm,
     handed, kg_ref, vg_ref,
-    qraw, graw, qs, gs, kall, vall, kt, bias, pst, dst, stag, zero, dsend, drecv, acc,
-    in_sem, own_sem, kv_send, kv_recv, dq_send, dq_recv, d_send, d_recv, zero_sem,
+    plan_ref, lens_ref, qraw, graw, qs, gs, kall, vall, kt, bias, pst, dst, stag, zero, term, dsend, drecv,
+    in_sem, own_sem, kv_send, kv_recv, dq_send, dq_recv, d_send, d_recv, zero_sem, table_sem,
 ):
     n_pp, n_cp, tokens, heads, nkv, hd, ndoc, groups, chunk = sizes
     group_heads = heads // nkv
@@ -30,55 +31,58 @@
     my_group = me // per_group
     scale = hd ** -0.5
 
-    q_in = pltpu.make_async_copy(q_hbm.at[0], qraw, in_sem.at[0])
-    g_in = pltpu.make_async_copy(g_hbm.at[0], graw, in_sem.at[1])
-    q_in.start()
-    g_in.start()
+    barrier = pltpu.get_barrier_semaphore()
+
+    @pl.when(me > 0)
+    def _():
+        pl.semaphore_signal(barrier, inc=1, device_id={"cp": me - 1}, device_id_type=MESH)
+
+    @pl.when(me < n_cp - 1)
+    def _():
+        pl.semaphore_signal(barrier, inc=1, device_id={"cp": me + 1}, device_id_type=MESH)
+
+    @pl.when(sec < n_pp - 1)
+    def _():
+        for d in range(n_cp):
+            pl.semaphore_signal(barrier, inc=1, device_id={"pp": sec + 1, "cp": d}, device_id_type=MESH)
+
+    plan_in = pltpu.make_async_copy(plan_hbm, plan_ref, table_sem.at[0])
+    lens_in = pltpu.make_async_copy(lens_hbm, lens_ref, table_sem.at[1])
     my_rows = pl.ds(pl.multiple_of(me * tokens, tokens), tokens)
     k_own = pltpu.make_async_copy(k_hbm.at[0], kall.at[my_rows], own_sem.at[0])
     v_own = pltpu.make_async_copy(v_hbm.at[0], vall.at[my_rows], own_sem.at[1])
-    k_own.start()
-    v_own.start()
-
-    barrier = pltpu.get_barrier_semaphore()
-    for d in range(n_cp):
-        @pl.when(me != d)
-        def _():
-            pl.semaphore_signal(barrier, inc=1, device_id={"cp": d}, device_id_type=MESH)
-
-        @pl.when(sec < n_pp - 1)
-        def _():
-            pl.semaphore_signal(barrier, inc=1, device_id={"pp": sec + 1, "cp": d}, device_id_type=MESH)
-
-    @pl.when(sec > 0)
-    def _():
-        pl.semaphore_wait(barrier, 2 * n_cp - 1)
-
-    @pl.when(sec == 0)
-    def _():
-        pl.semaphore_wait(barrier, n_cp - 1)
-
-    def kv_copies(d, source):
+    q_in = pltpu.make_async_copy(q_hbm.at[0], qraw, in_sem.at[0])
+    g_in = pltpu.make_async_copy(g_hbm.at[0], graw, in_sem.at[1])
+    for copy in (plan_in, lens_in, k_own, v_own, q_in, g_in):
+        copy.start()
+
+    neighbours = jnp.where(me > 0, 1, 0) + jnp.where(me < n_cp - 1, 1, 0)
+    pl.semaphore_wait(barrier, neighbours + jnp.where(sec > 0, n_cp, 0))
+
+    def kv_copies(source, own):
         rows = pl.ds(pl.multiple_of(source * tokens, tokens), tokens)
         return [
             pltpu.make_async_remote_copy(
-                src_ref=hbm.at[0], dst_ref=full.at[rows],
-                send_sem=kv_send.at[i, d], recv_sem=kv_recv.at[i, source],
-                device_id={"cp": d}, device_id_type=MESH,
+                src_ref=hbm.at[0] if own else full.at[rows], dst_ref=full.at[rows],
+                send_sem=kv_send.at[i, source], recv_sem=kv_recv.at[i, source],
+                device_id={"cp": lax.rem(me + 1, n_cp)}, device_id_type=MESH,
             )
             for i, (hbm, full) in enumerate(((k_hbm, kall), (v_hbm, vall)))
         ]
 
-    for d in reversed(range(n_cp)):
-        @pl.when((me != d) & (my_group <= d // per_group))
-        def _():
-            for copy in kv_copies(d, me):
-                copy.start()
+    @pl.when(me < n_cp - 1)
+    def _():
+        for copy in kv_copies(me, True):
+            copy.start()
 
     @pl.when(sec == n_pp - 1)
     def _():
         zero[...] = jnp.zeros_like(zero)
-        pltpu.make_async_copy(zero, handed.at[0], zero_sem).start()
+        for d in range(n_cp):
+            pltpu.make_async_copy(zero, handed.at[0, pl.ds(d * block_rows, block_rows)], zero_sem).start()
+
+    plan_in.wait()
+    lens_in.wait()
 
     def taken_of(slot):
         taken = jnp.zeros_like(slot)
@@ -136,23 +140,34 @@
             device_id={"pp": sec - 1, "cp": d}, device_id_type=MESH,
         )
 
-    def d_copy(kb, source, cols):
-        at = pl.ds(pl.multiple_of(source * tokens, tokens), tokens)
+    def d_copy(kb, kv, cols):
+        at = pl.ds(kb * tokens, tokens)
+        source = term if drecv.dtype == F32 else dsend
         return pltpu.make_async_remote_copy(
-            src_ref=dsend.at[pl.ds(kb * tokens, tokens), cols],
-            dst_ref=drecv.at[at, cols],
-            send_sem=d_send.at[kb], recv_sem=d_recv.at[source],
-            device_id={"cp": kb}, device_id_type=MESH,
+            src_ref=source.at[at, cols], dst_ref=drecv.at[at, cols],
+            send_sem=d_send.at[kb, kv], recv_sem=d_recv.at[kb, kv],
+            device_id={"cp": lax.rem(me + n_cp - 1, n_cp)}, device_id_type=MESH,
         )
+
+    for off in range(1, n_cp):
+        @pl.when(me >= off)
+        def _():
+            for copy in kv_copies(me - off, False):
+                copy.wait_recv()
+
+            @pl.when(me < n_cp - 1)
+            def _():
+                for copy in kv_copies(me - off, False):
+                    copy.start()
 
     def work(group):
         shards = (group + 1) * per_group
         count = shards * tokens
-        for s in range(shards):
-            @pl.when(me != s)
+        for s in range(group * per_group + 1, shards):
+            @pl.when(me < s)
             def _():
-                for copy in kv_copies(s, s):
-                    copy.wait_recv()
+                kall[s * tokens:(s + 1) * tokens, :] = jnp.zeros((tokens, kall.shape[1]), BF16)
+                vall[s * tokens:(s + 1) * tokens, :] = jnp.zeros((tokens, vall.shape[1]), BF16)
 
         def one_kv(kv, carry):
             kv_cols = pl.ds(pl.multiple_of(kv * hd, hd), hd)
@@ -201,16 +216,21 @@
                 at = slice(kb * tokens, (kb + 1) * tokens)
                 dkey = jnp.dot(dst[at, :], qs[all_rows, :], preferred_element_type=F32)
                 dvalue = jnp.dot(pst[at, :], gs[all_rows, :], preferred_element_type=F32)
-                both = jnp.concatenate([dkey, dvalue], axis=1)
-
-                @pl.when(me == kb)
+                term[at, term_cols] = jnp.concatenate([dkey, dvalue], axis=1)
+
+            for kb in range(shards):
+                at = slice(kb * tokens, (kb + 1) * tokens)
+
+                @pl.when((kb <= me) & (me < n_cp - 1))
                 def _():
-                    acc[:, term_cols] = both
-
-                @pl.when(me != kb)
+                    d_copy(kb, kv, term_cols).wait_recv()
+                    term[at, term_cols] += drecv[at, term_cols].astype(F32)
+
+                @pl.when(kb < me)
                 def _():
-                    dsend[at, term_cols] = both.astype(BF16)
-                    d_copy(kb, me, term_cols).start()
+                    if drecv.dtype != F32:
+                        dsend[at, term_cols] = term[at, term_cols].astype(BF16)
+                    d_copy(kb, kv, term_cols).start()
 
             return carry
 
@@ -222,26 +242,26 @@
     for group in range(groups):
         pl.when(my_group == group)(functools.partial(work, group))
 
-    everything = pl.ds(0, nkv * 2 * hd)
-    for s in range(n_cp):
-        @pl.when((me != s) & (my_group <= s // per_group))
+    for kv in range(nkv):
+        at = kv * 2 * hd
+        kg_ref[0, :, kv * hd:(kv + 1) * hd] = term[my_rows, at:at + hd].astype(BF16)
+        vg_ref[0, :, kv * hd:(kv + 1) * hd] = term[my_rows, at + hd:at + 2 * hd].astype(BF16)
+
+    @pl.when(me < n_cp - 1)
+    def _():
+        for copy in kv_copies(me, True):
+            copy.wait_send()
+
+    for s in range(n_cp - 1):
+        @pl.when((s < me) & (me < n_cp - 1))
         def _():
-            d_copy(0, s, everything).wait_recv()
-            acc[...] += drecv[s * tokens:(s + 1) * tokens, :].astype(F32)
-
-    for kv in range(nkv):
-        kg_ref[0, :, kv * hd:(kv + 1) * hd] = acc[:, kv * 2 * hd:kv * 2 * hd + hd].astype(BF16)
-        vg_ref[0, :, kv * hd:(kv + 1) * hd] = acc[:, kv * 2 * hd + hd:(kv + 1) * 2 * hd].astype(BF16)
-
-    for d in range(n_cp):
-        @pl.when((me != d) & (my_group <= d // per_group))
+            for copy in kv_copies(s, False):
+                copy.wait_send()
+
+        @pl.when(s < me)
         def _():
-            for copy in kv_copies(d, me):
-                copy.wait_send()
-
-        @pl.when((me != d) & (my_group >= d // per_group))
-        def _():
-            d_copy(d, me, everything).wait_send()
+            for kv in range(nkv):
+                d_copy(s, kv, pl.ds(kv * 2 * hd, 2 * hd)).wait_send()
 
     whole = pltpu.make_async_remote_copy(
         src_ref=stag, dst_ref=handed.at[0], send_sem=dq_send, recv_sem=dq_recv,
@@ -258,7 +278,16 @@
 
     @pl.when(sec == n_pp - 1)
     def _():
-        pltpu.make_async_copy(zero, handed.at[0], zero_sem).wait()
+        pltpu.make_async_copy(stag, handed.at[0], zero_sem).wait()
+
+
+def finish(handed, kg, vg, handed_out, kg_out, vg_out, sem):
+    pairs = ((handed, handed_out), (kg, kg_out), (vg, vg_out))
+    copies = [pltpu.make_async_copy(a, b, sem.at[i]) for i, (a, b) in enumerate(pairs)]
+    for copy in copies:
+        copy.start()
+    for copy in copies:
+        copy.wait()
 
 
 def body(n_pp, n_cp, n_tp, query, key, value, out_grad, lengths, plan):
@@ -273,9 +302,10 @@
     chunk = 4
     group_rows = heads // nkv * tokens
     sizes = (n_pp, n_cp, tokens, heads, nkv, hd, lengths.shape[0], groups, chunk)
+    hop = BF16 if n_cp <= 4 else F32
+    hbm = pl.BlockSpec(memory_space=pltpu.HBM)
     anywhere = pl.BlockSpec(memory_space=pl.ANY)
     vmem = pl.BlockSpec(memory_space=pltpu.VMEM)
-    smem = pl.BlockSpec(memory_space=pltpu.SMEM)
     dma = pltpu.SemaphoreType.DMA
     handed, key_grad, value_grad = pl.pallas_call(
         functools.partial(kernel, sizes),
@@ -284,9 +314,11 @@
             jax.ShapeDtypeStruct(key.shape, BF16),
             jax.ShapeDtypeStruct(value.shape, BF16),
         ),
-        in_specs=[smem, smem, anywhere, anywhere, anywhere, anywhere],
+        in_specs=[hbm] * 6,
         out_specs=(anywhere, vmem, vmem),
         scratch_shapes=[
+            pltpu.SMEM(plan.shape, jnp.int32),
+            pltpu.SMEM(lengths.shape, jnp.int32),
             pltpu.VMEM((tokens, width), BF16),
             pltpu.VMEM((tokens, width), BF16),
             pltpu.VMEM((heads * tokens, hd), BF16),
@@ -298,22 +330,32 @@
             pltpu.VMEM((seq, group_rows), BF16),
             pltpu.VMEM((seq, group_rows), BF16),
             pltpu.VMEM((tokens, width), wide),
-            pltpu.VMEM((tokens, width), wide),
-            pltpu.VMEM((seq, 2 * kv_width), BF16),
-            pltpu.VMEM((seq, 2 * kv_width), BF16),
-            pltpu.VMEM((tokens, 2 * kv_width), F32),
+            pltpu.VMEM((block_rows, width), wide),
+            pltpu.VMEM((seq, 2 * kv_width), F32),
+            pltpu.VMEM((seq, 2 * kv_width) if hop == BF16 else (16, 128), BF16),
+            pltpu.VMEM((seq, 2 * kv_width), hop),
             dma((2,)), dma((2,)), dma((2, n_cp)), dma((2, n_cp)),
-            dma, dma, dma((n_cp,)), dma((n_cp,)), dma,
+            dma, dma, dma((n_cp, nkv)), dma((n_cp, nkv)), dma, dma((2,)),
         ],
         compiler_params=pltpu.CompilerParams(
-            collective_id=0, has_side_effects=True, vmem_limit_bytes=(56 if seq > 512 else 32) * 2 ** 20
+            collective_id=0, has_side_effects=True, vmem_limit_bytes=VMEM
         ),
         cost_estimate=pl.CostEstimate(
             flops=10 * tokens * heads * seq * hd, bytes_accessed=6 * tokens * width,
             transcendentals=tokens * heads * seq,
         ),
     )(plan, lengths, query, key, value, out_grad)
-    return handed.astype(BF16), key_grad, value_grad
+    if wide != BF16:
+        return handed.astype(BF16), key_grad, value_grad
+    results = (handed, key_grad, value_grad)
+    return pl.pallas_call(
+        finish,
+        out_shape=tuple(jax.ShapeDtypeStruct(r.shape, r.dtype) for r in results),
+        in_specs=[anywhere] * 3,
+        out_specs=(hbm,) * 3,
+        scratch_shapes=[dma((3,))],
+        compiler_params=pltpu.CompilerParams(vmem_limit_bytes=VMEM),
+    )(*results)
 
 
 def solution(mesh):

time: 38.7 us -> 59.5 us (1.54)
  Pallas kernels: 30.7 us -> 58.7 us
  local copies, waits for them, and re-layouts: 6.95 us -> 0 us
    pallas_call x0 -> x1, Pallas kernels: none -> 19 us  [body(): pl.pallas_call(finish, out_shape=tuple((jax.ShapeDtypeStruct(r.shape, r.d...]
    pallas_call x1, Pallas kernels: 30.7 us -> 39.7 us  [body(): pl.pallas_call(functools.partial(kernel, sizes), out_shape=(jax.ShapeDtyp...]
    unnamed x15 -> x0, local copies, waits for them, and re-layouts: 6.95 us -> none
where the time goes in v2:
time: 59.5 us; the launch traced here: 59.3 us
  Pallas kernels  58.7 us (99%)
  between operations  0.64 us (1%)
    pallas_call x1, Pallas kernels, body(): pl.pallas_call(functools.partial(kernel, sizes), out_shape=(jax.ShapeDtyp...  39.7 us
    pallas_call x1, Pallas kernels, body(): pl.pallas_call(finish, out_shape=tuple((jax.ShapeDtypeStruct(r.shape, r.d...  19 us

profile of v2, /device:TPU:2, one launch (start us, length us, event | category | flops | bytes accessed | tf_op | source)
XLA Modules:
  0.0 59.3 jit_solution(5000854277225876292)
XLA Ops:
  0.6 39.7 %shard_map.85 = (bf16[1,128,2048]{2,1,0:T(8,128)(2,1)}, bf16[1,128,128]{2,1,0:T(8,128)(2,1)}, bf16[1,128,128]{2,1,0:T(8,128)(2,1)}) custom-call(s32[4,4]{1,0:T(4,128)} %plan_hbm.1, s32[6]{0:T(128)} %lens_hbm.1, bf16[1,128,2048]{2,1,0:T(8,128)(2,1)} %q_hbm.1, bf16[1,128,128]{2,1,0:T(8,128)(2,1)} %k_hbm.1, bf16[1,128,128]{2,1,0:T(8,128)(2,1)} %v_hbm.1, ...), custom_call_target="tpu_custom_call" | custom-call | flops 1342177280 | bytes 1572864 | tf_op jit(solution)/shard_map/pallas_call | solution.py:310
  40.3 19.0 %shard_map.86 = (bf16[1,128,2048]{2,1,0:T(8,128)(2,1)}, bf16[1,128,128]{2,1,0:T(8,128)(2,1)}, bf16[1,128,128]{2,1,0:T(8,128)(2,1)}) custom-call(bf16[1,128,2048]{2,1,0:T(8,128)(2,1)} %get-tuple-element.6.handed, bf16[1,128,128]{2,1,0:T(8,128)(2,1)} %get-tuple-element.7.kg, bf16[1,128,128]{2,1,0:T(8,128)(2,1)} %get-tuple-element.8.vg), custom_call_target="tpu_custom_call" | custom-call | tf_op jit(solution)/shard_map/pallas_call | solution.py:351

commit v3 on v1

--- a/solution.py
+++ b/solution.py
@@ -11,15 +11,16 @@
 MESH = pl.DeviceIdType.MESH
 F32 = jnp.float32
 BF16 = jnp.bfloat16
+VMEM = 60 * 2 ** 20
 NT = (((1,), (1,)), ((), ()))
 
 
 def kernel(
     sizes,
-    plan_ref, lens_ref, q_hbm, k_hbm, v_hbm, g_hbm,
+    plan_hbm, lens_hbm, q_hbm, k_hbm, v_hbm, g_hbm,
     handed, kg_ref, vg_ref,
-    qraw, graw, qs, gs, kall, vall, kt, bias, pst, dst, stag, zero, dsend, drecv, acc,
-    in_sem, own_sem, kv_send, kv_recv, dq_send, dq_recv, d_send, d_recv, zero_sem,
+    plan_ref, lens_ref, qraw, graw, qs, gs, kall, vall, kt, bias, pst, dst, stag, land, acc, dsend, drecv,
+    in_sem, own_sem, kv_send, kv_recv, dq_send, dq_recv, d_send, d_recv, out_sem, table_sem,
 ):
     n_pp, n_cp, tokens, heads, nkv, hd, ndoc, groups, chunk = sizes
     group_heads = heads // nkv
@@ -30,33 +31,29 @@
     my_group = me // per_group
     scale = hd ** -0.5
 
-    q_in = pltpu.make_async_copy(q_hbm.at[0], qraw, in_sem.at[0])
-    g_in = pltpu.make_async_copy(g_hbm.at[0], graw, in_sem.at[1])
-    q_in.start()
-    g_in.start()
+    barrier = pltpu.get_barrier_semaphore()
+
+    for d in range(n_cp):
+        @pl.when(me != d)
+        def _():
+            pl.semaphore_signal(barrier, inc=1, device_id={"cp": d}, device_id_type=MESH)
+
+    @pl.when(sec < n_pp - 1)
+    def _():
+        for d in range(n_cp):
+            pl.semaphore_signal(barrier, inc=1, device_id={"pp": sec + 1, "cp": d}, device_id_type=MESH)
+
+    plan_in = pltpu.make_async_copy(plan_hbm, plan_ref, table_sem.at[0])
+    lens_in = pltpu.make_async_copy(lens_hbm, lens_ref, table_sem.at[1])
     my_rows = pl.ds(pl.multiple_of(me * tokens, tokens), tokens)
     k_own = pltpu.make_async_copy(k_hbm.at[0], kall.at[my_rows], own_sem.at[0])
     v_own = pltpu.make_async_copy(v_hbm.at[0], vall.at[my_rows], own_sem.at[1])
-    k_own.start()
-    v_own.start()
-
-    barrier = pltpu.get_barrier_semaphore()
-    for d in range(n_cp):
-        @pl.when(me != d)
-        def _():
-            pl.semaphore_signal(barrier, inc=1, device_id={"cp": d}, device_id_type=MESH)
-
-        @pl.when(sec < n_pp - 1)
-        def _():
-            pl.semaphore_signal(barrier, inc=1, device_id={"pp": sec + 1, "cp": d}, device_id_type=MESH)
-
-    @pl.when(sec > 0)
-    def _():
-        pl.semaphore_wait(barrier, 2 * n_cp - 1)
-
-    @pl.when(sec == 0)
-    def _():
-        pl.semaphore_wait(barrier, n_cp - 1)
+    q_in = pltpu.make_async_copy(q_hbm.at[0], qraw, in_sem.at[0])
+    g_in = pltpu.make_async_copy(g_hbm.at[0], graw, in_sem.at[1])
+    for copy in (plan_in, lens_in, k_own, v_own, q_in, g_in):
+        copy.start()
+
+    pl.semaphore_wait(barrier, n_cp - 1 + jnp.where(sec > 0, n_cp, 0))
 
     def kv_copies(d, source):
         rows = pl.ds(pl.multiple_of(source * tokens, tokens), tokens)
@@ -77,8 +74,10 @@
 
     @pl.when(sec == n_pp - 1)
     def _():
-        zero[...] = jnp.zeros_like(zero)
-        pltpu.make_async_copy(zero, handed.at[0], zero_sem).start()
+        land[...] = jnp.zeros_like(land)
+
+    plan_in.wait()
+    lens_in.wait()
 
     def taken_of(slot):
         taken = jnp.zeros_like(slot)
@@ -128,12 +127,12 @@
     k_own.wait()
     v_own.wait()
 
-    def dq_copy(d, cols):
+    def dq_copy(d, piece):
         return pltpu.make_async_remote_copy(
-            src_ref=stag.at[pl.ds(d * block_rows, block_rows), cols],
-            dst_ref=handed.at[0, pl.ds(pl.multiple_of(me * block_rows, block_rows), block_rows), cols],
-            send_sem=dq_send, recv_sem=dq_recv,
-            device_id={"pp": sec - 1, "cp": d}, device_id_type=MESH,
+            src_ref=stag.at[piece, pl.ds(d * block_rows, block_rows)],
+            dst_ref=land.at[piece, pl.ds(pl.multiple_of(me * block_rows, block_rows), block_rows)],
+            send_sem=dq_send, recv_sem=dq_recv.at[piece],
+            device_id={"pp": lax.rem(sec + n_pp - 1, n_pp), "cp": d}, device_id_type=MESH,
         )
 
     def d_copy(kb, source, cols):
@@ -181,15 +180,13 @@
                     def _():
                         dqt = jnp.dot(kt[:, 0:count], dscore, preferred_element_type=F32)
                         for h in range(2):
-                            at = pl.ds(pl.multiple_of((kv * group_heads + first + h) * hd, hd), hd)
-                            stag[:, at] = dqt[:, h * tokens:(h + 1) * tokens].T.astype(stag.dtype)
+                            at = slice((pair * 2 + h) * hd, (pair * 2 + h + 1) * hd)
+                            stag[kv * (group_heads // chunk) + c, :, at] = dqt[:, h * tokens:(h + 1) * tokens].T.astype(stag.dtype)
 
                 @pl.when(sec > 0)
                 def _():
-                    width = chunk * hd
-                    cols = pl.ds(pl.multiple_of(kv * group_heads * hd + c * width, width), width)
                     for d in range(n_cp):
-                        dq_copy(d, cols).start()
+                        dq_copy(d, kv * (group_heads // chunk) + c).start()
 
                 return carry
 
@@ -243,22 +240,45 @@
         def _():
             d_copy(d, me, everything).wait_send()
 
-    whole = pltpu.make_async_remote_copy(
-        src_ref=stag, dst_ref=handed.at[0], send_sem=dq_send, recv_sem=dq_recv,
-        device_id={"pp": lax.rem(sec + 1, n_pp)}, device_id_type=MESH,
-    )
-
     @pl.when(sec > 0)
     def _():
-        whole.wait_send()
-
-    @pl.when(sec < n_pp - 1)
-    def _():
-        whole.wait_recv()
-
-    @pl.when(sec == n_pp - 1)
-    def _():
-        pltpu.make_async_copy(zero, handed.at[0], zero_sem).wait()
+        pltpu.make_async_remote_copy(
+            src_ref=stag, dst_ref=land, send_sem=dq_send, recv_sem=dq_recv.at[0],
+            device_id={"pp": lax.rem(sec + n_pp - 1, n_pp)}, device_id_type=MESH,
+        ).wait_send()
+
+    pieces = heads // chunk
+    outs = []
+    for piece in range(pieces):
+        @pl.when(sec < n_pp - 1)
+        def _():
+            pltpu.make_async_remote_copy(
+                src_ref=stag.at[piece], dst_ref=land.at[piece], send_sem=dq_send, recv_sem=dq_recv.at[piece],
+                device_id={"pp": lax.rem(sec + n_pp - 1, n_pp)}, device_id_type=MESH,
+            ).wait_recv()
+
+        cols = pl.ds(piece * chunk * hd, chunk * hd)
+        outs.append(pltpu.make_async_copy(land.at[piece], handed.at[0, :, cols], out_sem.at[piece]))
+        outs[-1].start()
+    for copy in outs:
+        copy.wait()
+
+
+def finish(handed, kg, vg, handed_out, kg_out, vg_out, handed_buf, kg_buf, vg_buf, sem):
+    rows = handed.shape[1] // 4
+    trips = [(kg, kg_buf, kg_out), (vg, vg_buf, vg_out)]
+    for i in range(4):
+        at = (slice(None), pl.ds(i * rows, rows))
+        trips.append((handed.at[at], handed_buf.at[at], handed_out.at[at]))
+    loads = [pltpu.make_async_copy(a, b, sem.at[0, i]) for i, (a, b, _) in enumerate(trips)]
+    stores = [pltpu.make_async_copy(b, c, sem.at[1, i]) for i, (_, b, c) in enumerate(trips)]
+    for load in loads:
+        load.start()
+    for load, store in zip(loads, stores):
+        load.wait()
+        store.start()
+    for store in stores:
+        store.wait()
 
 
 def body(n_pp, n_cp, n_tp, query, key, value, out_grad, lengths, plan):
@@ -273,9 +293,8 @@
     chunk = 4
     group_rows = heads // nkv * tokens
     sizes = (n_pp, n_cp, tokens, heads, nkv, hd, lengths.shape[0], groups, chunk)
-    anywhere = pl.BlockSpec(memory_space=pl.ANY)
+    hbm = pl.BlockSpec(memory_space=pltpu.HBM)
     vmem = pl.BlockSpec(memory_space=pltpu.VMEM)
-    smem = pl.BlockSpec(memory_space=pltpu.SMEM)
     dma = pltpu.SemaphoreType.DMA
     handed, key_grad, value_grad = pl.pallas_call(
         functools.partial(kernel, sizes),
@@ -284,9 +303,11 @@
             jax.ShapeDtypeStruct(key.shape, BF16),
             jax.ShapeDtypeStruct(value.shape, BF16),
         ),
-        in_specs=[smem, smem, anywhere, anywhere, anywhere, anywhere],
-        out_specs=(anywhere, vmem, vmem),
+        in_specs=[hbm] * 6,
+        out_specs=(hbm, vmem, vmem),
         scratch_shapes=[
+            pltpu.SMEM(plan.shape, jnp.int32),
+            pltpu.SMEM(lengths.shape, jnp.int32),
             pltpu.VMEM((tokens, width), BF16),
             pltpu.VMEM((tokens, width), BF16),
             pltpu.VMEM((heads * tokens, hd), BF16),
@@ -297,23 +318,33 @@
             pltpu.VMEM((seq, tokens), F32),
             pltpu.VMEM((seq, group_rows), BF16),
             pltpu.VMEM((seq, group_rows), BF16),
-            pltpu.VMEM((tokens, width), wide),
-            pltpu.VMEM((tokens, width), wide),
+            pltpu.VMEM((heads // chunk, tokens, chunk * hd), wide),
+            pltpu.VMEM((heads // chunk, tokens, chunk * hd), wide),
+            pltpu.VMEM((tokens, 2 * kv_width), F32),
             pltpu.VMEM((seq, 2 * kv_width), BF16),
             pltpu.VMEM((seq, 2 * kv_width), BF16),
-            pltpu.VMEM((tokens, 2 * kv_width), F32),
             dma((2,)), dma((2,)), dma((2, n_cp)), dma((2, n_cp)),
-            dma, dma, dma((n_cp,)), dma((n_cp,)), dma,
+            dma, dma((heads // chunk,)), dma((n_cp,)), dma((n_cp,)), dma((heads // chunk,)), dma((2,)),
         ],
         compiler_params=pltpu.CompilerParams(
-            collective_id=0, has_side_effects=True, vmem_limit_bytes=(56 if seq > 512 else 32) * 2 ** 20
+            collective_id=0, has_side_effects=True, vmem_limit_bytes=VMEM
         ),
         cost_estimate=pl.CostEstimate(
             flops=10 * tokens * heads * seq * hd, bytes_accessed=6 * tokens * width,
             transcendentals=tokens * heads * seq,
         ),
     )(plan, lengths, query, key, value, out_grad)
-    return handed.astype(BF16), key_grad, value_grad
+    if wide != BF16:
+        return handed.astype(BF16), key_grad, value_grad
+    results = (handed, key_grad, value_grad)
+    return pl.pallas_call(
+        finish,
+        out_shape=tuple(jax.ShapeDtypeStruct(r.shape, r.dtype) for r in results),
+        in_specs=[hbm] * 3,
+        out_specs=(hbm,) * 3,
+        scratch_shapes=[pltpu.VMEM(r.shape, r.dtype) for r in results] + [dma((2, 6))],
+        compiler_params=pltpu.CompilerParams(vmem_limit_bytes=VMEM),
+    )(*results)
 
 
 def solution(mesh):

time: 38.7 us -> 34.4 us (0.89)
  local copies, waits for them, and re-layouts: 6.95 us -> 0 us
  Pallas kernels: 30.7 us -> 33.7 us
    unnamed x15 -> x0, local copies, waits for them, and re-layouts: 6.95 us -> none
    pallas_call x0 -> x1, Pallas kernels: none -> 1.89 us  [body(): pl.pallas_call(finish, out_shape=tuple((jax.ShapeDtypeStruct(r.shape, r.d...]
    pallas_call x1, Pallas kernels: 30.7 us -> 31.8 us  [body(): pl.pallas_call(functools.partial(kernel, sizes), out_shape=(jax.ShapeDtyp...]
where the time goes in v3:
time: 34.4 us; the launch traced here: 34.3 us
  Pallas kernels  33.7 us (98%)
  between operations  0.64 us (2%)
    pallas_call x1, Pallas kernels, body(): pl.pallas_call(functools.partial(kernel, sizes), out_shape=(jax.ShapeDtyp...  31.8 us
    pallas_call x1, Pallas kernels, body(): pl.pallas_call(finish, out_shape=tuple((jax.ShapeDtypeStruct(r.shape, r.d...  1.89 us

profile of v3, /device:TPU:2, one launch (start us, length us, event | category | flops | bytes accessed | tf_op | source)
XLA Modules:
  0.0 34.3 jit_solution(15094648320231339281)
XLA Ops:
  0.6 31.8 %shard_map.85 = (bf16[1,128,2048]{2,1,0:T(8,128)(2,1)}, bf16[1,128,128]{2,1,0:T(8,128)(2,1)}, bf16[1,128,128]{2,1,0:T(8,128)(2,1)}) custom-call(s32[4,4]{1,0:T(4,128)} %plan_hbm.1, s32[6]{0:T(128)} %lens_hbm.1, bf16[1,128,2048]{2,1,0:T(8,128)(2,1)} %q_hbm.1, bf16[1,128,128]{2,1,0:T(8,128)(2,1)} %k_hbm.1, bf16[1,128,128]{2,1,0:T(8,128)(2,1)} %v_hbm.1, ...), custom_call_target="tpu_custom_call" | custom-call | flops 1342177280 | bytes 1572864 | tf_op jit(solution)/shard_map/pallas_call | solution.py:299
  32.4 1.9 %shard_map.86 = (bf16[1,128,2048]{2,1,0:T(8,128)(2,1)}, bf16[1,128,128]{2,1,0:T(8,128)(2,1)}, bf16[1,128,128]{2,1,0:T(8,128)(2,1)}) custom-call(bf16[1,128,2048]{2,1,0:T(8,128)(2,1)} %get-tuple-element.6.handed, bf16[1,128,128]{2,1,0:T(8,128)(2,1)} %get-tuple-element.7.kg, bf16[1,128,128]{2,1,0:T(8,128)(2,1)} %get-tuple-element.8.vg), custom_call_target="tpu_custom_call" | custom-call | tf_op jit(solution)/shard_map/pallas_call | solution.py:340

commit v4 on v3

--- a/solution.py
+++ b/solution.py
@@ -19,8 +19,8 @@
     sizes,
     plan_hbm, lens_hbm, q_hbm, k_hbm, v_hbm, g_hbm,
     handed, kg_ref, vg_ref,
-    plan_ref, lens_ref, qraw, graw, qs, gs, kall, vall, kt, bias, pst, dst, stag, land, acc, dsend, drecv,
-    in_sem, own_sem, kv_send, kv_recv, dq_send, dq_recv, d_send, d_recv, out_sem, table_sem,
+    plan_ref, lens_ref, qraw, graw, qs, gs, kall, vall, kt, bias, pst, dst, stag, land, relay, acc, dsend, drecv,
+    in_sem, own_sem, kv_send, kv_pass, kv_recv, dq_send, dq_recv, relay_send, relay_recv, d_send, d_recv, out_sem, table_sem,
 ):
     n_pp, n_cp, tokens, heads, nkv, hd, ndoc, groups, chunk = sizes
     group_heads = heads // nkv
@@ -55,21 +55,27 @@
 
     pl.semaphore_wait(barrier, n_cp - 1 + jnp.where(sec > 0, n_cp, 0))
 
-    def kv_copies(d, source):
+    def kv_copies(d, source, passed):
         rows = pl.ds(pl.multiple_of(source * tokens, tokens), tokens)
         return [
             pltpu.make_async_remote_copy(
-                src_ref=hbm.at[0], dst_ref=full.at[rows],
-                send_sem=kv_send.at[i, d], recv_sem=kv_recv.at[i, source],
+                src_ref=full.at[rows] if passed else hbm.at[0], dst_ref=full.at[rows],
+                send_sem=kv_pass.at[i, source] if passed else kv_send.at[i, d], recv_sem=kv_recv.at[i, source],
                 device_id={"cp": d}, device_id_type=MESH,
             )
             for i, (hbm, full) in enumerate(((k_hbm, kall), (v_hbm, vall)))
         ]
 
+    right = lax.rem(me + 1, n_cp)
+    passes = (me % 2 == 0) & (me < n_cp - 1)
+
+    def kv_to(d):
+        return me < d if d % 2 == 0 else me == d - 1
+
     for d in reversed(range(n_cp)):
-        @pl.when((me != d) & (my_group <= d // per_group))
-        def _():
-            for copy in kv_copies(d, me):
+        @pl.when(kv_to(d))
+        def _():
+            for copy in kv_copies(d, me, False):
                 copy.start()
 
     @pl.when(sec == n_pp - 1)
@@ -127,13 +133,58 @@
     k_own.wait()
     v_own.wait()
 
+    pieces = heads // chunk
+    relayed = pieces // 2
+    crosses = (sec > 0) & (sec % 2 == 0)
+    forwards = (sec % 2 == 1) & (sec < n_pp - 1)
+    before = lax.rem(sec + n_pp - 1, n_pp)
+    my_block = pl.ds(pl.multiple_of(me * block_rows, block_rows), block_rows)
+
     def dq_copy(d, piece):
         return pltpu.make_async_remote_copy(
-            src_ref=stag.at[piece, pl.ds(d * block_rows, block_rows)],
-            dst_ref=land.at[piece, pl.ds(pl.multiple_of(me * block_rows, block_rows), block_rows)],
+            src_ref=stag.at[piece, pl.ds(pl.multiple_of(d * block_rows, block_rows), block_rows)],
+            dst_ref=land.at[piece, my_block],
             send_sem=dq_send, recv_sem=dq_recv.at[piece],
-            device_id={"pp": lax.rem(sec + n_pp - 1, n_pp), "cp": d}, device_id_type=MESH,
+            device_id={"pp": before, "cp": d}, device_id_type=MESH,
         )
+
+    def cross_copy(off, piece):
+        d = lax.rem(me + off, n_cp)
+        return pltpu.make_async_remote_copy(
+            src_ref=stag.at[piece, pl.ds(pl.multiple_of(d * block_rows, block_rows), block_rows)],
+            dst_ref=relay.at[piece, pl.ds((off - 1) * block_rows, block_rows)],
+            send_sem=dq_send, recv_sem=relay_recv.at[piece],
+            device_id={"pp": before}, device_id_type=MESH,
+        )
+
+    def forward(piece):
+        pltpu.make_async_remote_copy(
+            src_ref=relay.at[piece], dst_ref=relay.at[piece], send_sem=dq_send, recv_sem=relay_recv.at[piece],
+            device_id={"pp": before}, device_id_type=MESH,
+        ).wait_recv()
+        for off in range(1, n_cp):
+            pltpu.make_async_remote_copy(
+                src_ref=relay.at[piece, pl.ds((off - 1) * block_rows, block_rows)],
+                dst_ref=land.at[piece, my_block],
+                send_sem=relay_send, recv_sem=dq_recv.at[piece],
+                device_id={"cp": lax.rem(me + off, n_cp)}, device_id_type=MESH,
+            ).start()
+
+    def send_dq(piece):
+        @pl.when(crosses & (piece < relayed))
+        def _():
+            for off in range(1, n_cp):
+                cross_copy(off, piece).start()
+            dq_copy(me, piece).start()
+
+        @pl.when((sec > 0) & jnp.logical_not(crosses & (piece < relayed)))
+        def _():
+            for d in range(n_cp):
+                dq_copy(d, piece).start()
+
+        @pl.when(forwards & (piece >= 1) & (piece <= relayed))
+        def _():
+            forward(piece - 1)
 
     def d_copy(kb, source, cols):
         at = pl.ds(pl.multiple_of(source * tokens, tokens), tokens)
@@ -144,14 +195,25 @@
             device_id={"cp": kb}, device_id_type=MESH,
         )
 
+    for s in range(n_cp - 1):
+        @pl.when(s < me)
+        def _():
+            for copy in kv_copies(right, s, True):
+                copy.wait_recv()
+
+            @pl.when(passes)
+            def _():
+                for copy in kv_copies(right, s, True):
+                    copy.start()
+
     def work(group):
         shards = (group + 1) * per_group
         count = shards * tokens
-        for s in range(shards):
-            @pl.when(me != s)
+        for s in range(group * per_group + 1, shards):
+            @pl.when(me < s)
             def _():
-                for copy in kv_copies(s, s):
-                    copy.wait_recv()
+                kall[s * tokens:(s + 1) * tokens, :] = jnp.zeros((tokens, kall.shape[1]), BF16)
+                vall[s * tokens:(s + 1) * tokens, :] = jnp.zeros((tokens, vall.shape[1]), BF16)
 
         def one_kv(kv, carry):
             kv_cols = pl.ds(pl.multiple_of(kv * hd, hd), hd)
@@ -183,11 +245,7 @@
                             at = slice((pair * 2 + h) * hd, (pair * 2 + h + 1) * hd)
                             stag[kv * (group_heads // chunk) + c, :, at] = dqt[:, h * tokens:(h + 1) * tokens].T.astype(stag.dtype)
 
-                @pl.when(sec > 0)
-                def _():
-                    for d in range(n_cp):
-                        dq_copy(d, kv * (group_heads // chunk) + c).start()
-
+                send_dq(kv * (group_heads // chunk) + c)
                 return carry
 
             lax.fori_loop(0, group_heads // chunk, one_chunk, 0)
@@ -204,7 +262,7 @@
                 def _():
                     acc[:, term_cols] = both
 
-                @pl.when(me != kb)
+                @pl.when(kb < me)
                 def _():
                     dsend[at, term_cols] = both.astype(BF16)
                     d_copy(kb, me, term_cols).start()
@@ -220,8 +278,8 @@
         pl.when(my_group == group)(functools.partial(work, group))
 
     everything = pl.ds(0, nkv * 2 * hd)
-    for s in range(n_cp):
-        @pl.when((me != s) & (my_group <= s // per_group))
+    for s in range(1, n_cp):
+        @pl.when(me < s)
         def _():
             d_copy(0, s, everything).wait_recv()
             acc[...] += drecv[s * tokens:(s + 1) * tokens, :].astype(F32)
@@ -231,14 +289,26 @@
         vg_ref[0, :, kv * hd:(kv + 1) * hd] = acc[:, kv * 2 * hd + hd:(kv + 1) * 2 * hd].astype(BF16)
 
     for d in range(n_cp):
-        @pl.when((me != d) & (my_group <= d // per_group))
-        def _():
-            for copy in kv_copies(d, me):
+        @pl.when(kv_to(d))
+        def _():
+            for copy in kv_copies(d, me, False):
                 copy.wait_send()
 
-        @pl.when((me != d) & (my_group >= d // per_group))
+        @pl.when((d < me) & passes)
+        def _():
+            for copy in kv_copies(right, d, True):
+                copy.wait_send()
+
+        @pl.when(d < me)
         def _():
             d_copy(d, me, everything).wait_send()
+
+    @pl.when(forwards)
+    def _():
+        pltpu.make_async_remote_copy(
+            src_ref=relay, dst_ref=relay, send_sem=relay_send, recv_sem=relay_recv.at[0],
+            device_id={"pp": before}, device_id_type=MESH,
+        ).wait_send()
 
     @pl.when(sec > 0)
     def _():
@@ -247,7 +317,6 @@
             device_id={"pp": lax.rem(sec + n_pp - 1, n_pp)}, device_id_type=MESH,
         ).wait_send()
 
-    pieces = heads // chunk
     outs = []
     for piece in range(pieces):
         @pl.when(sec < n_pp - 1)
@@ -320,11 +389,12 @@
             pltpu.VMEM((seq, group_rows), BF16),
             pltpu.VMEM((heads // chunk, tokens, chunk * hd), wide),
             pltpu.VMEM((heads // chunk, tokens, chunk * hd), wide),
+            pltpu.VMEM((heads // chunk // 2, tokens - block_rows, chunk * hd), wide),
             pltpu.VMEM((tokens, 2 * kv_width), F32),
             pltpu.VMEM((seq, 2 * kv_width), BF16),
             pltpu.VMEM((seq, 2 * kv_width), BF16),
-            dma((2,)), dma((2,)), dma((2, n_cp)), dma((2, n_cp)),
-            dma, dma((heads // chunk,)), dma((n_cp,)), dma((n_cp,)), dma((heads // chunk,)), dma((2,)),
+            dma((2,)), dma((2,)), dma((2, n_cp)), dma((2, n_cp)), dma((2, n_cp)),
+            dma, dma((heads // chunk,)), dma, dma((heads // chunk // 2,)), dma((n_cp,)), dma((n_cp,)), dma((heads // chunk,)), dma((2,)),
         ],
         compiler_params=pltpu.CompilerParams(
             collective_id=0, has_side_effects=True, vmem_limit_bytes=VMEM

time: 34.4 us -> 35.8 us (1.041)
  the two profiles are of different devices: /device:TPU:2 before, /device:TPU:1 now
where the time goes in v4:
time: 35.8 us; the launch traced here: 35.7 us
  Pallas kernels  35 us (98%)
  between operations  0.64 us (2%)
    pallas_call x1, Pallas kernels, body(): pl.pallas_call(functools.partial(kernel, sizes), out_shape=(jax.ShapeDtyp...  33.1 us
    pallas_call x1, Pallas kernels, body(): pl.pallas_call(finish, out_shape=tuple((jax.ShapeDtypeStruct(r.shape, r.d...  1.89 us

profile of v4, /device:TPU:1, one launch (start us, length us, event | category | flops | bytes accessed | tf_op | source)
XLA Modules:
  0.0 35.7 jit_solution(1720119668072540354)
XLA Ops:
  0.6 33.1 %shard_map.85 = (bf16[1,128,2048]{2,1,0:T(8,128)(2,1)}, bf16[1,128,128]{2,1,0:T(8,128)(2,1)}, bf16[1,128,128]{2,1,0:T(8,128)(2,1)}) custom-call(s32[4,4]{1,0:T(4,128)} %plan_hbm.1, s32[6]{0:T(128)} %lens_hbm.1, bf16[1,128,2048]{2,1,0:T(8,128)(2,1)} %q_hbm.1, bf16[1,128,128]{2,1,0:T(8,128)(2,1)} %k_hbm.1, bf16[1,128,128]{2,1,0:T(8,128)(2,1)} %v_hbm.1, ...), custom_call_target="tpu_custom_call" | custom-call | flops 1342177280 | bytes 1572864 | tf_op jit(solution)/shard_map/pallas_call | solution.py:368
  33.8 1.9 %shard_map.86 = (bf16[1,128,2048]{2,1,0:T(8,128)(2,1)}, bf16[1,128,128]{2,1,0:T(8,128)(2,1)}, bf16[1,128,128]{2,1,0:T(8,128)(2,1)}) custom-call(bf16[1,128,2048]{2,1,0:T(8,128)(2,1)} %get-tuple-element.6.handed, bf16[1,128,128]{2,1,0:T(8,128)(2,1)} %get-tuple-element.7.kg, bf16[1,128,128]{2,1,0:T(8,128)(2,1)} %get-tuple-element.8.vg), custom_call_target="tpu_custom_call" | custom-call | tf_op jit(solution)/shard_map/pallas_call | solution.py:410

commit v5 on v4

--- a/solution.py
+++ b/solution.py
@@ -181,10 +181,6 @@
         def _():
             for d in range(n_cp):
                 dq_copy(d, piece).start()
-
-        @pl.when(forwards & (piece >= 1) & (piece <= relayed))
-        def _():
-            forward(piece - 1)
 
     def d_copy(kb, source, cols):
         at = pl.ds(pl.multiple_of(source * tokens, tokens), tokens)
@@ -249,6 +245,11 @@
                 return carry
 
             lax.fori_loop(0, group_heads // chunk, one_chunk, 0)
+
+            for piece in range(relayed):
+                @pl.when(forwards & (kv == piece * chunk * nkv // heads))
+                def _():
+                    forward(piece)
 
             all_rows = pl.ds(pl.multiple_of(kv * group_heads * tokens, group_heads * tokens), group_heads * tokens)
             term_cols = pl.ds(pl.multiple_of(kv * 2 * hd, 2 * hd), 2 * hd)

time: 35.8 us -> 33.8 us (0.944)
  Pallas kernels: 35 us -> 33 us
    pallas_call x1, Pallas kernels: 33.1 us -> 31.2 us  [body(): pl.pallas_call(functools.partial(kernel, sizes), out_shape=(jax.ShapeDtyp...]
where the time goes in v5:
time: 33.8 us; the launch traced here: 33.7 us
  Pallas kernels  33 us (98%)
  between operations  0.64 us (2%)
    pallas_call x1, Pallas kernels, body(): pl.pallas_call(functools.partial(kernel, sizes), out_shape=(jax.ShapeDtyp...  31.2 us
    pallas_call x1, Pallas kernels, body(): pl.pallas_call(finish, out_shape=tuple((jax.ShapeDtypeStruct(r.shape, r.d...  1.89 us

profile of v5, /device:TPU:1, one launch (start us, length us, event | category | flops | bytes accessed | tf_op | source)
XLA Modules:
  0.0 33.7 jit_solution(9393109857898030403)
XLA Ops:
  0.6 31.2 %shard_map.85 = (bf16[1,128,2048]{2,1,0:T(8,128)(2,1)}, bf16[1,128,128]{2,1,0:T(8,128)(2,1)}, bf16[1,128,128]{2,1,0:T(8,128)(2,1)}) custom-call(s32[4,4]{1,0:T(4,128)} %plan_hbm.1, s32[6]{0:T(128)} %lens_hbm.1, bf16[1,128,2048]{2,1,0:T(8,128)(2,1)} %q_hbm.1, bf16[1,128,128]{2,1,0:T(8,128)(2,1)} %k_hbm.1, bf16[1,128,128]{2,1,0:T(8,128)(2,1)} %v_hbm.1, ...), custom_call_target="tpu_custom_call" | custom-call | flops 1342177280 | bytes 1572864 | tf_op jit(solution)/shard_map/pallas_call | solution.py:369
  31.8 1.9 %shard_map.86 = (bf16[1,128,2048]{2,1,0:T(8,128)(2,1)}, bf16[1,128,128]{2,1,0:T(8,128)(2,1)}, bf16[1,128,128]{2,1,0:T(8,128)(2,1)}) custom-call(bf16[1,128,2048]{2,1,0:T(8,128)(2,1)} %get-tuple-element.6.handed, bf16[1,128,128]{2,1,0:T(8,128)(2,1)} %get-tuple-element.7.kg, bf16[1,128,128]{2,1,0:T(8,128)(2,1)} %get-tuple-element.8.vg), custom_call_target="tpu_custom_call" | custom-call | tf_op jit(solution)/shard_map/pallas_call | solution.py:411

commit v6 on v5

--- a/solution.py
+++ b/solution.py
@@ -20,7 +20,7 @@
     plan_hbm, lens_hbm, q_hbm, k_hbm, v_hbm, g_hbm,
     handed, kg_ref, vg_ref,
     plan_ref, lens_ref, qraw, graw, qs, gs, kall, vall, kt, bias, pst, dst, stag, land, relay, acc, dsend, drecv,
-    in_sem, own_sem, kv_send, kv_pass, kv_recv, dq_send, dq_recv, relay_send, relay_recv, d_send, d_recv, out_sem, table_sem,
+    in_sem, own_sem, kv_send, kv_recv, dq_send, dq_recv, relay_send, relay_recv, d_send, d_recv, out_sem, table_sem,
 ):
     n_pp, n_cp, tokens, heads, nkv, hd, ndoc, groups, chunk = sizes
     group_heads = heads // nkv
@@ -55,27 +55,21 @@
 
     pl.semaphore_wait(barrier, n_cp - 1 + jnp.where(sec > 0, n_cp, 0))
 
-    def kv_copies(d, source, passed):
+    def kv_copies(d, source):
         rows = pl.ds(pl.multiple_of(source * tokens, tokens), tokens)
         return [
             pltpu.make_async_remote_copy(
-                src_ref=full.at[rows] if passed else hbm.at[0], dst_ref=full.at[rows],
-                send_sem=kv_pass.at[i, source] if passed else kv_send.at[i, d], recv_sem=kv_recv.at[i, source],
+                src_ref=hbm.at[0], dst_ref=full.at[rows],
+                send_sem=kv_send.at[i, d], recv_sem=kv_recv.at[i, source],
                 device_id={"cp": d}, device_id_type=MESH,
             )
             for i, (hbm, full) in enumerate(((k_hbm, kall), (v_hbm, vall)))
         ]
 
-    right = lax.rem(me + 1, n_cp)
-    passes = (me % 2 == 0) & (me < n_cp - 1)
-
-    def kv_to(d):
-        return me < d if d % 2 == 0 else me == d - 1
-
-    for d in reversed(range(n_cp)):
-        @pl.when(kv_to(d))
-        def _():
-            for copy in kv_copies(d, me, False):
+    for d in reversed(range(1, n_cp)):
+        @pl.when(me < d)
+        def _():
+            for copy in kv_copies(d, me):
                 copy.start()
 
     @pl.when(sec == n_pp - 1)
@@ -194,13 +188,8 @@
     for s in range(n_cp - 1):
         @pl.when(s < me)
         def _():
-            for copy in kv_copies(right, s, True):
+            for copy in kv_copies(n_cp - 1, s):
                 copy.wait_recv()
-
-            @pl.when(passes)
-            def _():
-                for copy in kv_copies(right, s, True):
-                    copy.start()
 
     def work(group):
         shards = (group + 1) * per_group
@@ -290,14 +279,9 @@
         vg_ref[0, :, kv * hd:(kv + 1) * hd] = acc[:, kv * 2 * hd + hd:(kv + 1) * 2 * hd].astype(BF16)
 
     for d in range(n_cp):
-        @pl.when(kv_to(d))
-        def _():
-            for copy in kv_copies(d, me, False):
-                copy.wait_send()
-
-        @pl.when((d < me) & passes)
-        def _():
-            for copy in kv_copies(right, d, True):
+        @pl.when(me < d)
+        def _():
+            for copy in kv_copies(d, me):
                 copy.wait_send()
 
         @pl.when(d < me)
@@ -394,7 +378,7 @@
             pltpu.VMEM((tokens, 2 * kv_width), F32),
             pltpu.VMEM((seq, 2 * kv_width), BF16),
             pltpu.VMEM((seq, 2 * kv_width), BF16),
-            dma((2,)), dma((2,)), dma((2, n_cp)), dma((2, n_cp)), dma((2, n_cp)),
+            dma((2,)), dma((2,)), dma((2, n_cp)), dma((2, n_cp)),
             dma, dma((heads // chunk,)), dma, dma((heads // chunk // 2,)), dma((n_cp,)), dma((n_cp,)), dma((heads // chunk,)), dma((2,)),
         ],
         compiler_params=pltpu.CompilerParams(

time: 33.8 us -> 33.2 us (0.982)
  Pallas kernels: 33 us -> 32.4 us
    pallas_call x1, Pallas kernels: 31.2 us -> 30.5 us  [body(): pl.pallas_call(functools.partial(kernel, sizes), out_shape=(jax.ShapeDtyp...]
where the time goes in v6:
time: 33.2 us; the launch traced here: 33.1 us
  Pallas kernels  32.4 us (98%)
  between operations  0.64 us (2%)
    pallas_call x1, Pallas kernels, body(): pl.pallas_call(functools.partial(kernel, sizes), out_shape=(jax.ShapeDtyp...  30.5 us
    pallas_call x1, Pallas kernels, body(): pl.pallas_call(finish, out_shape=tuple((jax.ShapeDtypeStruct(r.shape, r.d...  1.89 us

profile of v6, /device:TPU:1, one launch (start us, length us, event | category | flops | bytes accessed | tf_op | source)
XLA Modules:
  0.0 33.1 jit_solution(14333332859924119968)
XLA Ops:
  0.6 30.5 %shard_map.85 = (bf16[1,128,2048]{2,1,0:T(8,128)(2,1)}, bf16[1,128,128]{2,1,0:T(8,128)(2,1)}, bf16[1,128,128]{2,1,0:T(8,128)(2,1)}) custom-call(s32[4,4]{1,0:T(4,128)} %plan_hbm.1, s32[6]{0:T(128)} %lens_hbm.1, bf16[1,128,2048]{2,1,0:T(8,128)(2,1)} %q_hbm.1, bf16[1,128,128]{2,1,0:T(8,128)(2,1)} %k_hbm.1, bf16[1,128,128]{2,1,0:T(8,128)(2,1)} %v_hbm.1, ...), custom_call_target="tpu_custom_call" | custom-call | flops 1342177280 | bytes 1572864 | tf_op jit(solution)/shard_map/pallas_call | solution.py:353
  31.2 1.9 %shard_map.86 = (bf16[1,128,2048]{2,1,0:T(8,128)(2,1)}, bf16[1,128,128]{2,1,0:T(8,128)(2,1)}, bf16[1,128,128]{2,1,0:T(8,128)(2,1)}) custom-call(bf16[1,128,2048]{2,1,0:T(8,128)(2,1)} %get-tuple-element.6.handed, bf16[1,128,128]{2,1,0:T(8,128)(2,1)} %get-tuple-element.7.kg, bf16[1,128,128]{2,1,0:T(8,128)(2,1)} %get-tuple-element.8.vg), custom_call_target="tpu_custom_call" | custom-call | tf_op jit(solution)/shard_map/pallas_call | solution.py:395

commit v7 on v6

--- a/solution.py
+++ b/solution.py
@@ -20,7 +20,7 @@
     plan_hbm, lens_hbm, q_hbm, k_hbm, v_hbm, g_hbm,
     handed, kg_ref, vg_ref,
     plan_ref, lens_ref, qraw, graw, qs, gs, kall, vall, kt, bias, pst, dst, stag, land, relay, acc, dsend, drecv,
-    in_sem, own_sem, kv_send, kv_recv, dq_send, dq_recv, relay_send, relay_recv, d_send, d_recv, out_sem, table_sem,
+    in_sem, own_sem, kv_send, kv_pass, kv_recv, dq_send, dq_recv, relay_send, relay_recv, d_send, d_recv, out_sem, table_sem,
 ):
     n_pp, n_cp, tokens, heads, nkv, hd, ndoc, groups, chunk = sizes
     group_heads = heads // nkv
@@ -66,11 +66,26 @@
             for i, (hbm, full) in enumerate(((k_hbm, kall), (v_hbm, vall)))
         ]
 
+    def kv_direct(d):
+        return (me < d) & (me != d - 2) if d % 2 else me < d
+
     for d in reversed(range(1, n_cp)):
-        @pl.when(me < d)
+        @pl.when(kv_direct(d))
         def _():
             for copy in kv_copies(d, me):
                 copy.start()
+
+    odd = me % 2
+    passes = (odd == 0) & (me >= 2) & (me < n_cp - 1)
+    passed_rows = pl.ds(pl.multiple_of(lax.rem(me + n_cp - 1, n_cp) * tokens, tokens), tokens)
+    kv_passed = [
+        pltpu.make_async_remote_copy(
+            src_ref=full.at[passed_rows], dst_ref=full.at[passed_rows],
+            send_sem=kv_pass.at[i], recv_sem=kv_recv.at[i, lax.rem(me + n_cp - 1, n_cp)],
+            device_id={"cp": lax.rem(me + 1, n_cp)}, device_id_type=MESH,
+        )
+        for i, full in enumerate((kall, vall))
+    ]
 
     @pl.when(sec == n_pp - 1)
     def _():
@@ -176,20 +191,34 @@
             for d in range(n_cp):
                 dq_copy(d, piece).start()
 
-    def d_copy(kb, source, cols):
-        at = pl.ds(pl.multiple_of(source * tokens, tokens), tokens)
+    def d_copy(kb):
+        slot = odd * kb + (1 - odd) * me
+        target = odd * (me - 1) + (1 - odd) * kb
         return pltpu.make_async_remote_copy(
-            src_ref=dsend.at[pl.ds(kb * tokens, tokens), cols],
-            dst_ref=drecv.at[at, cols],
-            send_sem=d_send.at[kb], recv_sem=d_recv.at[source],
-            device_id={"cp": kb}, device_id_type=MESH,
+            src_ref=dsend.at[pl.ds(kb * tokens, tokens)],
+            dst_ref=drecv.at[pl.ds(pl.multiple_of(slot * tokens, tokens), tokens)],
+            send_sem=d_send.at[kb], recv_sem=d_recv.at[slot],
+            device_id={"cp": target}, device_id_type=MESH,
         )
 
-    for s in range(n_cp - 1):
+    def d_arrived(slot):
+        at = pl.ds(slot * tokens, tokens)
+        pltpu.make_async_remote_copy(
+            src_ref=dsend.at[at], dst_ref=drecv.at[at], send_sem=d_send.at[slot], recv_sem=d_recv.at[slot],
+            device_id={"cp": lax.rem(me + 1, n_cp)}, device_id_type=MESH,
+        ).wait_recv()
+        return drecv[slot * tokens:(slot + 1) * tokens, :].astype(F32)
+
+    for s in reversed(range(n_cp - 1)):
         @pl.when(s < me)
         def _():
             for copy in kv_copies(n_cp - 1, s):
                 copy.wait_recv()
+
+        @pl.when(passes & (s == me - 1))
+        def _():
+            for copy in kv_passed:
+                copy.start()
 
     def work(group):
         shards = (group + 1) * per_group
@@ -255,7 +284,11 @@
                 @pl.when(kb < me)
                 def _():
                     dsend[at, term_cols] = both.astype(BF16)
-                    d_copy(kb, me, term_cols).start()
+
+                if nkv == 1:
+                    @pl.when((kb < me) & (odd == 1))
+                    def _():
+                        d_copy(kb).start()
 
             return carry
 
@@ -267,26 +300,43 @@
     for group in range(groups):
         pl.when(my_group == group)(functools.partial(work, group))
 
-    everything = pl.ds(0, nkv * 2 * hd)
-    for s in range(1, n_cp):
-        @pl.when(me < s)
-        def _():
-            d_copy(0, s, everything).wait_recv()
-            acc[...] += drecv[s * tokens:(s + 1) * tokens, :].astype(F32)
+    for kb in range(n_cp - 1):
+        at = slice(kb * tokens, (kb + 1) * tokens)
+
+        @pl.when((kb < me) & (odd == 0))
+        def _():
+            dsend[at, :] = (dsend[at, :].astype(F32) + d_arrived(kb)).astype(BF16)
+            d_copy(kb).start()
+
+        if nkv > 1:
+            @pl.when((kb < me) & (odd == 1))
+            def _():
+                d_copy(kb).start()
+
+    for e in range(0, n_cp, 2):
+        @pl.when(me <= e)
+        def _():
+            acc[...] += d_arrived(e)
 
     for kv in range(nkv):
         kg_ref[0, :, kv * hd:(kv + 1) * hd] = acc[:, kv * 2 * hd:kv * 2 * hd + hd].astype(BF16)
         vg_ref[0, :, kv * hd:(kv + 1) * hd] = acc[:, kv * 2 * hd + hd:(kv + 1) * 2 * hd].astype(BF16)
 
     for d in range(n_cp):
-        @pl.when(me < d)
-        def _():
-            for copy in kv_copies(d, me):
-                copy.wait_send()
+        if d > 0:
+            @pl.when(kv_direct(d))
+            def _():
+                for copy in kv_copies(d, me):
+                    copy.wait_send()
 
         @pl.when(d < me)
         def _():
-            d_copy(d, me, everything).wait_send()
+            d_copy(d).wait_send()
+
+    @pl.when(passes)
+    def _():
+        for copy in kv_passed:
+            copy.wait_send()
 
     @pl.when(forwards)
     def _():
@@ -378,7 +428,7 @@
             pltpu.VMEM((tokens, 2 * kv_width), F32),
             pltpu.VMEM((seq, 2 * kv_width), BF16),
             pltpu.VMEM((seq, 2 * kv_width), BF16),
-            dma((2,)), dma((2,)), dma((2, n_cp)), dma((2, n_cp)),
+            dma((2,)), dma((2,)), dma((2, n_cp)), dma((2,)), dma((2, n_cp)),
             dma, dma((heads // chunk,)), dma, dma((heads // chunk // 2,)), dma((n_cp,)), dma((n_cp,)), dma((heads // chunk,)), dma((2,)),
         ],
         compiler_params=pltpu.CompilerParams(

time: 33.2 us -> 35 us (1.054)
  Pallas kernels: 32.4 us -> 34.2 us
    pallas_call x1, Pallas kernels: 30.5 us -> 32.3 us  [body(): pl.pallas_call(functools.partial(kernel, sizes), out_shape=(jax.ShapeDtyp...]
where the time goes in v7:
time: 35 us; the launch traced here: 34.8 us
  Pallas kernels  34.2 us (98%)
  between operations  0.64 us (2%)
    pallas_call x1, Pallas kernels, body(): pl.pallas_call(functools.partial(kernel, sizes), out_shape=(jax.ShapeDtyp...  32.3 us
    pallas_call x1, Pallas kernels, body(): pl.pallas_call(finish, out_shape=tuple((jax.ShapeDtypeStruct(r.shape, r.d...  1.89 us

profile of v7, /device:TPU:1, one launch (start us, length us, event | category | flops | bytes accessed | tf_op | source)
XLA Modules:
  0.0 34.8 jit_solution(6230565619264900019)
XLA Ops:
  0.6 32.3 %shard_map.85 = (bf16[1,128,2048]{2,1,0:T(8,128)(2,1)}, bf16[1,128,128]{2,1,0:T(8,128)(2,1)}, bf16[1,128,128]{2,1,0:T(8,128)(2,1)}) custom-call(s32[4,4]{1,0:T(4,128)} %plan_hbm.1, s32[6]{0:T(128)} %lens_hbm.1, bf16[1,128,2048]{2,1,0:T(8,128)(2,1)} %q_hbm.1, bf16[1,128,128]{2,1,0:T(8,128)(2,1)} %k_hbm.1, bf16[1,128,128]{2,1,0:T(8,128)(2,1)} %v_hbm.1, ...), custom_call_target="tpu_custom_call" | custom-call | flops 1342177280 | bytes 1572864 | tf_op jit(solution)/shard_map/pallas_call | solution.py:403
  32.9 1.9 %shard_map.86 = (bf16[1,128,2048]{2,1,0:T(8,128)(2,1)}, bf16[1,128,128]{2,1,0:T(8,128)(2,1)}, bf16[1,128,128]{2,1,0:T(8,128)(2,1)}) custom-call(bf16[1,128,2048]{2,1,0:T(8,128)(2,1)} %get-tuple-element.6.handed, bf16[1,128,128]{2,1,0:T(8,128)(2,1)} %get-tuple-element.7.kg, bf16[1,128,128]{2,1,0:T(8,128)(2,1)} %get-tuple-element.8.vg), custom_call_target="tpu_custom_call" | custom-call | tf_op jit(solution)/shard_map/pallas_call | solution.py:445

commit v8 on v7

--- a/solution.py
+++ b/solution.py
@@ -20,7 +20,7 @@
     plan_hbm, lens_hbm, q_hbm, k_hbm, v_hbm, g_hbm,
     handed, kg_ref, vg_ref,
     plan_ref, lens_ref, qraw, graw, qs, gs, kall, vall, kt, bias, pst, dst, stag, land, relay, acc, dsend, drecv,
-    in_sem, own_sem, kv_send, kv_pass, kv_recv, dq_send, dq_recv, relay_send, relay_recv, d_send, d_recv, out_sem, table_sem,
+    in_sem, own_sem, kv_send, kv_recv, dq_send, dq_recv, relay_send, relay_recv, d_send, d_recv, out_sem, table_sem,
 ):
     n_pp, n_cp, tokens, heads, nkv, hd, ndoc, groups, chunk = sizes
     group_heads = heads // nkv
@@ -66,26 +66,13 @@
             for i, (hbm, full) in enumerate(((k_hbm, kall), (v_hbm, vall)))
         ]
 
-    def kv_direct(d):
-        return (me < d) & (me != d - 2) if d % 2 else me < d
-
     for d in reversed(range(1, n_cp)):
-        @pl.when(kv_direct(d))
+        @pl.when(me < d)
         def _():
             for copy in kv_copies(d, me):
                 copy.start()
 
     odd = me % 2
-    passes = (odd == 0) & (me >= 2) & (me < n_cp - 1)
-    passed_rows = pl.ds(pl.multiple_of(lax.rem(me + n_cp - 1, n_cp) * tokens, tokens), tokens)
-    kv_passed = [
-        pltpu.make_async_remote_copy(
-            src_ref=full.at[passed_rows], dst_ref=full.at[passed_rows],
-            send_sem=kv_pass.at[i], recv_sem=kv_recv.at[i, lax.rem(me + n_cp - 1, n_cp)],
-            device_id={"cp": lax.rem(me + 1, n_cp)}, device_id_type=MESH,
-        )
-        for i, full in enumerate((kall, vall))
-    ]
 
     @pl.when(sec == n_pp - 1)
     def _():
@@ -209,16 +196,11 @@
         ).wait_recv()
         return drecv[slot * tokens:(slot + 1) * tokens, :].astype(F32)
 
-    for s in reversed(range(n_cp - 1)):
+    for s in range(n_cp - 1):
         @pl.when(s < me)
         def _():
             for copy in kv_copies(n_cp - 1, s):
                 copy.wait_recv()
-
-        @pl.when(passes & (s == me - 1))
-        def _():
-            for copy in kv_passed:
-                copy.start()
 
     def work(group):
         shards = (group + 1) * per_group
@@ -323,20 +305,14 @@
         vg_ref[0, :, kv * hd:(kv + 1) * hd] = acc[:, kv * 2 * hd + hd:(kv + 1) * 2 * hd].astype(BF16)
 
     for d in range(n_cp):
-        if d > 0:
-            @pl.when(kv_direct(d))
-            def _():
-                for copy in kv_copies(d, me):
-                    copy.wait_send()
+        @pl.when(me < d)
+        def _():
+            for copy in kv_copies(d, me):
+                copy.wait_send()
 
         @pl.when(d < me)
         def _():
             d_copy(d).wait_send()
-
-    @pl.when(passes)
-    def _():
-        for copy in kv_passed:
-            copy.wait_send()
 
     @pl.when(forwards)
     def _():
@@ -428,7 +404,7 @@
             pltpu.VMEM((tokens, 2 * kv_width), F32),
             pltpu.VMEM((seq, 2 * kv_width), BF16),
             pltpu.VMEM((seq, 2 * kv_width), BF16),
-            dma((2,)), dma((2,)), dma((2, n_cp)), dma((2,)), dma((2, n_cp)),
+            dma((2,)), dma((2,)), dma((2, n_cp)), dma((2, n_cp)),
             dma, dma((heads // chunk,)), dma, dma((heads // chunk // 2,)), dma((n_cp,)), dma((n_cp,)), dma((heads // chunk,)), dma((2,)),
         ],
         compiler_params=pltpu.CompilerParams(

time: 35 us -> 31.7 us (0.906)
  Pallas kernels: 34.2 us -> 30.9 us
    pallas_call x1, Pallas kernels: 32.3 us -> 29 us  [body(): pl.pallas_call(functools.partial(kernel, sizes), out_shape=(jax.ShapeDtyp...]
where the time goes in v8:
time: 31.7 us; the launch traced here: 31.5 us
  Pallas kernels  30.9 us (97%)
  between operations  0.64 us (2%)
    pallas_call x1, Pallas kernels, body(): pl.pallas_call(functools.partial(kernel, sizes), out_shape=(jax.ShapeDtyp...  29 us
    pallas_call x1, Pallas kernels, body(): pl.pallas_call(finish, out_shape=tuple((jax.ShapeDtypeStruct(r.shape, r.d...  1.89 us

profile of v8, /device:TPU:1, one launch (start us, length us, event | category | flops | bytes accessed | tf_op | source)
XLA Modules:
  0.0 31.5 jit_solution(12237108529333028794)
XLA Ops:
  0.6 29.0 %shard_map.85 = (bf16[1,128,2048]{2,1,0:T(8,128)(2,1)}, bf16[1,128,128]{2,1,0:T(8,128)(2,1)}, bf16[1,128,128]{2,1,0:T(8,128)(2,1)}) custom-call(s32[4,4]{1,0:T(4,128)} %plan_hbm.1, s32[6]{0:T(128)} %lens_hbm.1, bf16[1,128,2048]{2,1,0:T(8,128)(2,1)} %q_hbm.1, bf16[1,128,128]{2,1,0:T(8,128)(2,1)} %k_hbm.1, bf16[1,128,128]{2,1,0:T(8,128)(2,1)} %v_hbm.1, ...), custom_call_target="tpu_custom_call" | custom-call | flops 1342177280 | bytes 1572864 | tf_op jit(solution)/shard_map/pallas_call | solution.py:379
  29.6 1.9 %shard_map.86 = (bf16[1,128,2048]{2,1,0:T(8,128)(2,1)}, bf16[1,128,128]{2,1,0:T(8,128)(2,1)}, bf16[1,128,128]{2,1,0:T(8,128)(2,1)}) custom-call(bf16[1,128,2048]{2,1,0:T(8,128)(2,1)} %get-tuple-element.6.handed, bf16[1,128,128]{2,1,0:T(8,128)(2,1)} %get-tuple-element.7.kg, bf16[1,128,128]{2,1,0:T(8,128)(2,1)} %get-tuple-element.8.vg), custom_call_target="tpu_custom_call" | custom-call | tf_op jit(solution)/shard_map/pallas_call | solution.py:421

commit v9 on v8

--- a/solution.py
+++ b/solution.py
@@ -177,6 +177,10 @@
         def _():
             for d in range(n_cp):
                 dq_copy(d, piece).start()
+
+        @pl.when(forwards & (piece >= 2) & (piece < relayed + 2))
+        def _():
+            forward(piece - 2)
 
     def d_copy(kb):
         slot = odd * kb + (1 - odd) * me
@@ -245,11 +249,6 @@
                 return carry
 
             lax.fori_loop(0, group_heads // chunk, one_chunk, 0)
-
-            for piece in range(relayed):
-                @pl.when(forwards & (kv == piece * chunk * nkv // heads))
-                def _():
-                    forward(piece)
 
             all_rows = pl.ds(pl.multiple_of(kv * group_heads * tokens, group_heads * tokens), group_heads * tokens)
             term_cols = pl.ds(pl.multiple_of(kv * 2 * hd, 2 * hd), 2 * hd)

time: 31.7 us -> 32.7 us (1.032)
  Pallas kernels: 30.9 us -> 32 us
    pallas_call x1, Pallas kernels: 29 us -> 30.1 us  [body(): pl.pallas_call(functools.partial(kernel, sizes), out_shape=(jax.ShapeDtyp...]
where the time goes in v9:
time: 32.7 us; the launch traced here: 32.6 us
  Pallas kernels  32 us (98%)
  between operations  0.64 us (2%)
    pallas_call x1, Pallas kernels, body(): pl.pallas_call(functools.partial(kernel, sizes), out_shape=(jax.ShapeDtyp...  30.1 us
    pallas_call x1, Pallas kernels, body(): pl.pallas_call(finish, out_shape=tuple((jax.ShapeDtypeStruct(r.shape, r.d...  1.89 us

profile of v9, /device:TPU:1, one launch (start us, length us, event | category | flops | bytes accessed | tf_op | source)
XLA Modules:
  0.0 32.6 jit_solution(7025577599411382185)
XLA Ops:
  0.6 30.1 %shard_map.85 = (bf16[1,128,2048]{2,1,0:T(8,128)(2,1)}, bf16[1,128,128]{2,1,0:T(8,128)(2,1)}, bf16[1,128,128]{2,1,0:T(8,128)(2,1)}) custom-call(s32[4,4]{1,0:T(4,128)} %plan_hbm.1, s32[6]{0:T(128)} %lens_hbm.1, bf16[1,128,2048]{2,1,0:T(8,128)(2,1)} %q_hbm.1, bf16[1,128,128]{2,1,0:T(8,128)(2,1)} %k_hbm.1, bf16[1,128,128]{2,1,0:T(8,128)(2,1)} %v_hbm.1, ...), custom_call_target="tpu_custom_call" | custom-call | flops 1342177280 | bytes 1572864 | tf_op jit(solution)/shard_map/pallas_call | solution.py:378
  30.7 1.9 %shard_map.86 = (bf16[1,128,2048]{2,1,0:T(8,128)(2,1)}, bf16[1,128,128]{2,1,0:T(8,128)(2,1)}, bf16[1,128,128]{2,1,0:T(8,128)(2,1)}) custom-call(bf16[1,128,2048]{2,1,0:T(8,128)(2,1)} %get-tuple-element.6.handed, bf16[1,128,128]{2,1,0:T(8,128)(2,1)} %get-tuple-element.7.kg, bf16[1,128,128]{2,1,0:T(8,128)(2,1)} %get-tuple-element.8.vg), custom_call_target="tpu_custom_call" | custom-call | tf_op jit(solution)/shard_map/pallas_call | solution.py:420
